TPU v7x, 256 devices: a whole 4x4x8 slice. The times are simulated.
256 devices in a mesh: seq: 32 (over y, x, core), mp: 8 (over z).
Axes of the slice: x: 4, y: 4, z: 8, core: 2. Of those that a mesh axis runs over, the one named last changes fastest.
Arguments:
- hidden_rows: bfloat16 [4096, 8192], P('seq', 'mp'), may hold values from -6 to 6
- rotated_queries: bfloat16 [4096, 8192], P('seq', 'mp'), may hold values from -80 to 80
- rotated_keys: bfloat16 [4096, 1024], P('seq', 'mp'), may hold values from -6 to 6
- value_rows: bfloat16 [4096, 1024], P('seq', 'mp'), may hold values from -6 to 6
- adapter_down: bfloat16 [32, 16, 8192], P(None, None, 'mp'), may hold values from -0.0625 to 0.0625
- adapter_up: bfloat16 [32, 16, 8192], P(None, None, 'mp'), may hold values from -1.5 to 1.5
- output_gradient: bfloat16 [4096, 8192], P('seq', 'mp'), may hold values from -6 to 6
- document_blocks: int32 [9], replicated, may hold values from 1 to 17, 32 in all
- document_adapter: int32 [9], replicated, may hold values from 0 to 31
Outputs:
- attn_out: bfloat16 [4096, 8192], P('seq', 'mp')
- grad_q: bfloat16 [4096, 8192], P('seq', 'mp')
- grad_k: bfloat16 [4096, 1024], P('seq', 'mp')
- grad_v: bfloat16 [4096, 1024], P('seq', 'mp')
- grad_a: float32 [32, 16, 8192], P('seq', None, 'mp')
- grad_b: float32 [32, 16, 8192], P('seq', None, 'mp')
All inputs are finite; a program needn't handle non-finite values.
Results may differ from a plain program's by a relative error of at most 0.02.
Values may be sent and summed in bfloat16 or wider, within the bound.
A program may use at most 128 MiB of HBM per device.

v0:
```python
import math

import jax
import jax.numpy as jnp
from jax import lax
from jax.sharding import PartitionSpec as P

HEAD_WIDTH = 128


def block_documents(document_blocks, count):
    ends = jnp.cumsum(document_blocks)
    blocks = jnp.arange(count, dtype=jnp.int32)
    return jnp.sum((blocks[:, None] >= ends[None, :]).astype(jnp.int32), axis=1)


def pick(table, index):
    places = jnp.arange(table.shape[0], dtype=jnp.int32)
    return jnp.sum(jnp.where(places == index, table, 0))


def window_mask(same, rows):
    places = jnp.arange(rows, dtype=jnp.int32)
    causal = places[None, :] <= places[:, None]
    parts = [jnp.logical_and(causal, same[0])]
    for dist in range(1, same.shape[0]):
        parts.append(jnp.broadcast_to(same[dist], (rows, rows)))
    return jnp.concatenate(parts, axis=1)


def attend(query, window, allowed, output_gradient, scale):
    rows = query.shape[0]
    kv_cols = window.shape[2]
    groups = kv_cols // HEAD_WIDTH
    ratio = query.shape[1] // kv_cols
    q_four = query.reshape(rows, groups, ratio, HEAD_WIDTH)
    keys = window[:, 0].reshape(-1, groups, HEAD_WIDTH)
    values = window[:, 1].reshape(-1, groups, HEAD_WIDTH)
    scores = jnp.einsum("tgjd,ugd->gjtu", q_four, keys, preferred_element_type=jnp.float32) * scale
    scores = jnp.where(allowed[None, None], scores, -1e30)
    top = jnp.max(scores, axis=-1, keepdims=True)
    lse = top + jnp.log(jnp.sum(jnp.exp(scores - top), axis=-1, keepdims=True))
    probs = jnp.exp(scores - lse)
    probs_b = probs.astype(jnp.bfloat16)
    out = jnp.einsum("gjtu,ugd->tgjd", probs_b, values, preferred_element_type=jnp.float32).astype(
        jnp.bfloat16
    )
    grad_four = output_gradient.reshape(rows, groups, ratio, HEAD_WIDTH)
    delta = jnp.sum(grad_four.astype(jnp.float32) * out.astype(jnp.float32), axis=-1)
    delta = jnp.transpose(delta, (1, 2, 0))[..., None]
    dprob = jnp.einsum("tgjd,ugd->gjtu", grad_four, values, preferred_element_type=jnp.float32)
    dscore = (probs * (dprob - delta)).astype(jnp.bfloat16)
    grad_query = (
        jnp.einsum("gjtu,ugd->tgjd", dscore, keys, preferred_element_type=jnp.float32) * scale
    ).astype(jnp.bfloat16)
    grad_keys = (
        jnp.einsum("gjtu,tgjd->ugd", dscore, q_four, preferred_element_type=jnp.float32) * scale
    )
    grad_values = jnp.einsum(
        "gjtu,tgjd->ugd", probs_b, grad_four, preferred_element_type=jnp.float32
    )
    both = jnp.stack((grad_keys.reshape(-1, kv_cols), grad_values.reshape(-1, kv_cols)), axis=1)
    return (out.reshape(rows, -1), grad_query.reshape(rows, -1), both)


def on_device(
    hidden_rows,
    rotated_queries,
    rotated_keys,
    value_rows,
    adapter_down,
    adapter_up,
    output_gradient,
    document_blocks,
    document_adapter,
):
    scale = 1.0 / math.sqrt(HEAD_WIDTH)
    rows = hidden_rows.shape[0]
    count = lax.axis_size("seq")
    reach = count // 2 + 1
    own = lax.axis_index("seq")
    docs = block_documents(document_blocks, count)
    doc_own = pick(docs, own)
    adapter_index = pick(document_adapter, doc_own)
    down_rows = lax.dynamic_index_in_dim(adapter_down, adapter_index, 0, keepdims=False)
    up_rows = lax.dynamic_index_in_dim(adapter_up, adapter_index, 0, keepdims=False)
    low_part = lax.dot_general(
        hidden_rows, down_rows, (((1,), (1,)), ((), ())), preferred_element_type=jnp.float32
    )
    low = lax.psum(low_part, "mp").astype(jnp.bfloat16)
    query = (
        rotated_queries.astype(jnp.float32)
        + jnp.dot(low, up_rows, preferred_element_type=jnp.float32)
    ).astype(jnp.bfloat16)
    kv_rows = jnp.stack((rotated_keys, value_rows), axis=1)
    same = []
    for dist in range(reach):
        other = own - dist
        same.append(jnp.logical_and(other >= 0, pick(docs, other) == doc_own))
    allowed = window_mask(jnp.stack(same), rows)
    pieces = [kv_rows]
    whole = lax.all_gather(kv_rows, "seq", axis=0, tiled=True)
    for dist in range(1, reach):
        start = jnp.maximum(own - dist, 0) * rows
        pieces.append(lax.dynamic_slice_in_dim(whole, start, rows, 0))
    window = jnp.concatenate(pieces, axis=0)
    attn_out, grad_q, both = attend(query, window, allowed, output_gradient, scale)
    buffer = jnp.zeros((rows * count, 2, kv_rows.shape[2]), jnp.float32)
    for dist in range(reach):
        start = jnp.maximum(own - dist, 0) * rows
        part = lax.dynamic_slice_in_dim(buffer, start, rows, 0)
        buffer = lax.dynamic_update_slice_in_dim(
            buffer, part + both[dist * rows : (dist + 1) * rows], start, 0
        )
    total = lax.psum_scatter(
        buffer.astype(jnp.bfloat16), "seq", scatter_dimension=0, tiled=True
    ).astype(jnp.float32)
    grad_k = total[:, 0].astype(jnp.bfloat16)
    grad_v = total[:, 1].astype(jnp.bfloat16)
    dlow_part = lax.dot_general(
        grad_q, up_rows, (((1,), (1,)), ((), ())), preferred_element_type=jnp.float32
    )
    dlow = lax.psum(dlow_part, "mp").astype(jnp.bfloat16)
    grad_up = jnp.dot(low.T, grad_q, preferred_element_type=jnp.float32)
    grad_down = jnp.dot(dlow.T, hidden_rows, preferred_element_type=jnp.float32)
    chosen_adapter = (jnp.arange(adapter_down.shape[0], dtype=jnp.int32) == adapter_index)[
        :, None, None
    ]
    terms_down = jnp.where(chosen_adapter, grad_down[None], 0.0)
    terms_up = jnp.where(chosen_adapter, grad_up[None], 0.0)
    grad_a, grad_b = (
        lax.psum_scatter(
            terms_down.astype(jnp.bfloat16), "seq", scatter_dimension=0, tiled=True
        ).astype(jnp.float32),
        lax.psum_scatter(
            terms_up.astype(jnp.bfloat16), "seq", scatter_dimension=0, tiled=True
        ).astype(jnp.float32),
    )
    return (attn_out, grad_q, grad_k, grad_v, grad_a, grad_b)


def solution(mesh):
    return jax.shard_map(
        on_device,
        mesh=mesh,
        in_specs=(
            P("seq", "mp"),
            P("seq", "mp"),
            P("seq", "mp"),
            P("seq", "mp"),
            P(None, None, "mp"),
            P(None, None, "mp"),
            P("seq", "mp"),
            P(),
            P(),
        ),
        out_specs=(
            P("seq", "mp"),
            P("seq", "mp"),
            P("seq", "mp"),
            P("seq", "mp"),
            P("seq", None, "mp"),
            P("seq", None, "mp"),
        ),
        check_vma=False,
    )
```

profile of v0, /device:TPU:1, one launch (start us, length us, event | category | flops | bytes accessed | tf_op | source)
XLA Modules:
  0.0 374.9 jit_solution(5328389750946263330)
XLA Ops:
  7.2 1.5 pad_maximum_fusion.1
  9.0 1.1 copy.49
  10.0 0.8 reduce-window.8
  11.0 1.0 fusion.98
  32.0 1.9 fusion.99
  35.9 1.2 convolution_bitcast_fusion.2
  37.1 17.7 %psum.14 = bf16[128,16]{0,1:T(8,128)(2,1)S(1)} all-reduce(f32[128,16]{0,1:T(8,128)S(1)} %convolution_bitcast_fusion.2), channel_id=1, replica_groups=mesh['seq'=32,'mp'=8] {'mp'}, use_global_device_ids=true, to_apply=%region_20.21 | all-reduce | flops 2048 | bytes 12288 | tf_op jit(solution)/shard_map/psum | solution.py:90
  55.9 1.2 fusion.7
  57.1 7.2 %all-gather.2.cloned.1.call-done = bf16[4096,2,128]{2,0,1:T(8,128)(2,1)} async-done(((bf16[128,2,128]{2,0,1:T(8,128)(2,1)}), bf16[4096,2,128]{2,0,1:T(8,128)(2,1)}) %all-gather.2.cloned.1.call-update) | async-done | bytes 2097168 | tf_op jit(solution)/shard_map/all_gather | solution.py:102
  64.3 0.9 constant_dynamic-update-slice_fusion.15
  65.2 0.9 constant_dynamic-update-slice_fusion.14
  66.0 0.9 constant_dynamic-update-slice_fusion.13
  66.9 0.9 constant_dynamic-update-slice_fusion.12
  67.8 0.9 constant_dynamic-update-slice_fusion.11
  68.6 0.9 constant_dynamic-update-slice_fusion.10
  69.5 0.9 constant_dynamic-update-slice_fusion.9
  70.3 0.9 constant_dynamic-update-slice_fusion.8
  71.2 0.9 constant_dynamic-update-slice_fusion.7
  72.1 0.9 constant_dynamic-update-slice_fusion.6
  72.9 0.9 constant_dynamic-update-slice_fusion.5
  73.8 0.9 constant_dynamic-update-slice_fusion.4
  74.7 0.9 constant_dynamic-update-slice_fusion.3
  75.5 0.9 constant_dynamic-update-slice_fusion.2
  76.4 0.9 constant_dynamic-update-slice_fusion.1
  77.3 0.9 constant_dynamic-update-slice_fusion
  78.1 1.4 fusion.100
  79.5 1.2 exponential_reduce_fusion
  80.7 2.4 multiply_reduce_fusion
  83.2 2.2 fusion.3
  85.4 0.8 fusion.8
  86.2 1.3 copy-done.2
  87.8 14.1 %psum.15 = bf16[128,16]{0,1:T(8,128)(2,1)S(1)} all-reduce(f32[128,16]{0,1:T(8,128)S(1)} %fusion.67), channel_id=1, replica_groups=mesh['seq'=32,'mp'=8] {'mp'}, use_global_device_ids=true, to_apply=%region_25.26 | all-reduce | flops 2048 | bytes 12288 | tf_op jit(solution)/shard_map/psum | solution.py:123
  102.1 1.9 select_convert_fusion
  104.1 6.9 %copy.52 = bf16[8,128,2176]{2,0,1:T(8,128)(2,1)} copy(bf16[8,128,2176]{1,2,0:T(8,128)(2,1)} %copy-done.2) | data formatting | bytes 8912896 | tf_op jit(solution)/shard_map/reshape.27
  111.0 3.1 fusion.6
  114.2 5.0 %convolution_bitcast_fusion = f32[2176,1,128]{0,2,1:T(8,128)S(1)} fusion(f32[1,8,128,2176]{2,3,1,0:T(8,128)} %copy-done.1, f32[8,128]{1,0:T(8,128)S(1)} %log_add_fusion, bf16[128,1024]{1,0:T(8,128)(2,1)S(1)} %copy-done.4), kind=kOutput, calls=%fused_computation.41 | convolution fusion | flops 574881792 | bytes 10293248 | tf_op jit(solution)/shard_map/gjtu,tgjd->ugd/dot_general | solution.py:59
  119.2 2.4 broadcast_in_dim.148
  122.3 1.6 fusion.61
  123.8 1.6 fusion.59
  125.5 1.6 fusion.57
  127.1 1.6 fusion.55
  128.7 1.6 fusion.53
  130.3 1.6 fusion.51
  131.9 1.6 fusion.49
  133.4 1.6 fusion.47
  135.0 1.6 fusion.45
  136.6 1.6 fusion.43
  138.2 1.6 fusion.41
  139.8 1.6 fusion.39
  141.4 1.6 fusion.37
  143.0 1.6 fusion.35
  144.6 1.6 fusion.63
  146.1 1.6 fusion.65
  147.7 2.5 convert_element_type.95
  150.2 2.5 copy.69
  152.7 0.9 copy.56
  153.6 0.8 copy.55
  154.5 32.9 %reduce-scatter.6.cloned.1.call-done = bf16[1,16,1024]{2,1,0:T(8,128)(2,1)} async-done(((bf16[32,16,1024]{2,1,0:T(8,128)(2,1)}), bf16[1,16,1024]{2,1,0:T(8,128)(2,1)}) %reduce-scatter.6.cloned.1.call-update) | async-done | bytes 32784 | tf_op jit(solution)/shard_map/reduce_scatter | solution.py:132
  187.4 1.4 convert_element_type.100
  188.8 87.5 %reduce-scatter.8.cloned.1.call-done = bf16[1,16,1024]{2,1,0:T(8,128)(2,1)} async-done(((bf16[32,16,1024]{2,1,0:T(8,128)(2,1)}), bf16[1,16,1024]{2,1,0:T(8,128)(2,1)}) %reduce-scatter.8.cloned.1.call-update) | async-done | bytes 32784 | tf_op jit(solution)/shard_map/reduce_scatter | solution.py:135
  276.3 1.4 convert_element_type.102
  277.7 88.2 %reduce-scatter.10.cloned.1.call-done = bf16[128,256]{1,0:T(8,128)(2,1)} async-done(((bf16[4096,256]{1,0:T(8,128)(2,1)}), bf16[128,256]{1,0:T(8,128)(2,1)}) %reduce-scatter.10.cloned.1.call-update) | async-done | bytes 65552
  365.9 0.9 copy.70
  366.9 0.7 copy.57
  (48 shorter events, 3.3 us)
Async XLA Ops:
  7.2 48.7 %copy-start = (bf16[32,16,1024]{2,1,0:T(8,128)(2,1)S(1)}, bf16[32,16,1024]{2,1,0:T(8,128)(2,1)}, u32[]{:S(2)}) copy-start(bf16[32,16,1024]{2,1,0:T(8,128)(2,1)} %param.14) | copy-start | bytes 3145732
  7.2 57.1 %all-gather.2.cloned.1.call-start = ((), (), s32[]{:S(2)}) async-start(), calls=%async_computation.3 | async-start | bytes 2162688 | tf_op jit(solution)/shard_map/all_gather | solution.py:102
  8.8 178.7 %reduce-scatter.6.cloned.1.call-start = ((), (), s32[]{:S(2)}) async-start(), calls=%async_computation.4 | async-start | bytes 1081344 | tf_op jit(solution)/shard_map/reduce_scatter | solution.py:132
  79.5 3.6 copy-start.1
  80.7 2.4 copy-start.3
  85.3 2.1 copy-start.2
  85.3 16.6 %copy-start.6 = (bf16[128,1024]{1,0:T(8,128)(2,1)S(1)}, bf16[128,1024]{1,0:T(8,128)(2,1)}, u32[]{:S(2)}) copy-start(bf16[128,1024]{1,0:T(8,128)(2,1)} %param.9) | copy-start | bytes 786436
  104.0 172.4 %reduce-scatter.8.cloned.1.call-start = ((), (), s32[]{:S(2)}) async-start(), calls=%async_computation.5 | async-start | bytes 1081344 | tf_op jit(solution)/shard_map/reduce_scatter | solution.py:135
  111.0 3.1 copy-start.4
  125.5 240.4 %reduce-scatter.10.cloned.1.call-start = ((), (), s32[]{:S(2)}) async-start(), calls=%async_computation.6 | async-start | bytes 2162688
  152.7 0.9 copy-start.5
Sparse Core Ops, SparseCore 0:
  11.2 53.0 all-gather.1
  104.1 83.2 reduce-scatter.5
  191.7 84.5 reduce-scatter.7
  280.0 85.8 reduce-scatter.9
where the time goes:
time: 377 us; the launch traced here: 375 us
  waiting for transfers between devices  216 us (57%)
  other arithmetic  40.3 us (11%)
  between operations  36.2 us (10%)
  local copies, waits for them, and re-layouts  32.5 us (9%)
  blocking collectives  31.8 us (8%)
  matrix products  17.8 us (5%)
    unnamed x5, waiting for transfers between devices  88.2 us
    reduce_scatter x1, waiting for transfers between devices, on_device(): lax.psum_scatter(terms_up.astype(jnp.bfloat16), 'seq', scatter_dimension=...  87.5 us
    reduce_scatter x1, waiting for transfers between devices, on_device(): lax.psum_scatter(terms_down.astype(jnp.bfloat16), 'seq', scatter_dimensio...  32.9 us
    dynamic_update_slice x17, other arithmetic, on_device(): lax.dynamic_update_slice_in_dim(buffer, part + both[dist * rows:(dist + 1...  26 us
    unnamed x51, local copies, waits for them, and re-layouts  21.2 us
    psum x1, blocking collectives, on_device(): low = lax.psum(low_part, 'mp').astype(jnp.bfloat16)  17.7 us
    psum x1, blocking collectives, on_device(): dlow = lax.psum(dlow_part, 'mp').astype(jnp.bfloat16)  14.1 us
  transfers between devices with their start and end apart: 4, of which 4 were waited for; matrix products, arithmetic and copies ran while one was open for 16% of the time, Pallas kernels for 0%

commit v1 on v0

v1 whole, which is shorter than its diff:
```python
import functools
import math

import jax
import jax.numpy as jnp
from jax import lax
from jax.experimental import pallas as pl
from jax.experimental.pallas import tpu as pltpu
from jax.sharding import PartitionSpec as P

HEAD = 128
BLK = 128
RANK = 16
CHUNK = 256
NEG = -1e30
LOG2E = 1.4426950408889634
MESH = pl.DeviceIdType.MESH
F32 = jnp.float32
BF16 = jnp.bfloat16

NT = (((1,), (1,)), ((), ()))


def dot(a, b):
    return jnp.dot(a, b, preferred_element_type=F32)


def dot_nt(a, b):
    return lax.dot_general(a, b, NT, preferred_element_type=F32)


def kernel(
    seq, mp, docs,
    db, da, hid_h, rq_h, k_h, v_h, down_h, up_h, do_h,
    out_h, gq_h, gk_h, gv_h, ga_h, gb_h,
    hid, rq, down, up, do, kv, qs, dos, sbuf, dpbuf,
    lowx, dlowx, stat, ot, dqt, outv, gqv, pair, own_st, sib_out, sib_in,
    dkv_out, dkv_in, gkv, select, piece, got, red, fin, gout,
    load_sem, out_sem,
    low_send, low_recv, dlow_send, dlow_recv,
    kv_send, kv_recv, fwd_send, fwd_recv, sib_send, sib_recv, dkv_send, dkv_recv,
    a1_send, a1_recv, a2_send, a2_recv,
):
    reach = seq // 4
    chips = seq // 2
    cols = hid.shape[1]
    heads = cols // HEAD
    chunks = cols // CHUNK
    per = CHUNK // HEAD
    scale = 1.0 / math.sqrt(HEAD)
    fold = scale * LOG2E

    own = lax.axis_index("seq")
    m = lax.axis_index("mp")
    chip = own // 2
    core = own % 2
    sib = own + 1 - 2 * core
    mine = pl.ds(pl.multiple_of(core * BLK, BLK), BLK)
    other = pl.ds(pl.multiple_of((1 - core) * BLK, BLK), BLK)

    def load(src, dst, n):
        return pltpu.make_async_copy(src, dst, load_sem.at[n])

    loads = [
        load(k_h, kv.at[0, 0, mine], 0),
        load(v_h, kv.at[0, 1, mine], 1),
        load(hid_h, hid, 2),
        load(down_h, down, 3),
        load(up_h, up, 4),
        load(rq_h, rq, 5),
        load(do_h, do, 6),
    ]
    for one in loads:
        one.start()

    barrier = pltpu.get_barrier_semaphore()

    @pl.loop(1, seq)
    def _(step):
        pl.semaphore_signal(
            barrier, inc=1, device_id=((own + step) % seq, m), device_id_type=MESH
        )

    for step in range(1, mp):
        pl.semaphore_signal(
            barrier, inc=1, device_id=(own, (m + step) % mp), device_id_type=MESH
        )

    start = jnp.int32(0)
    first = jnp.int32(0)
    adapter = jnp.int32(0)
    bounds = []
    for d in range(docs):
        end = start + db[d]
        inside = jnp.logical_and(own >= start, own < end)
        first = jnp.where(inside, start, first)
        adapter = jnp.where(inside, da[d], adapter)
        bounds.append((start, end, da[d]))
        start = end

    loads[2].wait()
    loads[3].wait()
    lowx[m] = dot_nt(down[adapter], hid[...])
    loads[0].wait()
    loads[1].wait()

    pl.semaphore_wait(barrier, seq - 1 + mp - 1)

    def exchange(buf, send, recv):
        copies = []
        for step in range(1, mp):
            peer = (m + step) % mp
            copies.append(
                pltpu.make_async_remote_copy(
                    src_ref=buf.at[m], dst_ref=buf.at[m],
                    send_sem=send.at[step], recv_sem=recv.at[step],
                    device_id=(own, peer), device_id_type=MESH,
                )
            )
        return copies

    low_copies = exchange(lowx, low_send, low_recv)
    for one in low_copies:
        one.start()

    def kv_copy(e):
        return pltpu.make_async_remote_copy(
            src_ref=kv.at[0, :, mine], dst_ref=kv.at[e, :, mine],
            send_sem=kv_send.at[e], recv_sem=kv_recv.at[e],
            device_id=(own + 2 * e, m), device_id_type=MESH,
        )

    def kv_land(e):
        return pltpu.make_async_remote_copy(
            src_ref=kv.at[0, :, mine], dst_ref=kv.at[e, :, mine],
            send_sem=kv_send.at[e], recv_sem=kv_recv.at[e],
            device_id=(sib, m), device_id_type=MESH,
        )

    def forward(e):
        return pltpu.make_async_remote_copy(
            src_ref=kv.at[e, :, mine], dst_ref=kv.at[e, :, mine],
            send_sem=fwd_send.at[e], recv_sem=fwd_recv.at[e],
            device_id=(sib, m), device_id_type=MESH,
        )

    def forward_land(e):
        return pltpu.make_async_remote_copy(
            src_ref=kv.at[e, :, other], dst_ref=kv.at[e, :, other],
            send_sem=fwd_send.at[e], recv_sem=fwd_recv.at[e],
            device_id=(sib, m), device_id_type=MESH,
        )

    later = jnp.minimum(reach, chips - 1 - chip)
    earlier = jnp.minimum(reach, chip)

    forward(0).start()

    @pl.loop(1, later + 1)
    def _(e):
        kv_copy(e).start()

    loads[6].wait()
    for h in range(heads):
        dos[h * BLK : (h + 1) * BLK, :] = do[:, h * HEAD : (h + 1) * HEAD]

    wide = seq * 8
    row = lax.broadcasted_iota(jnp.int32, (wide, wide), 0)
    col = lax.broadcasted_iota(jnp.int32, (wide, wide), 1)
    same = (row % 8) == (col % 8)
    row_a = row // 8
    col_s = col // 8
    hit = jnp.zeros((wide, wide), F32)
    for begin, end, name in bounds:
        inside = jnp.logical_and(col_s >= begin, col_s < end)
        inside = jnp.logical_and(inside, row_a == name)
        hit = jnp.where(jnp.logical_and(inside, same), 1.0, hit)
    select[...] = hit.astype(BF16)

    loads[4].wait()
    loads[5].wait()
    for one in low_copies:
        one.wait_recv()
    low_sum = lowx[0]
    for step in range(1, mp):
        low_sum = low_sum + lowx[step]
    low_t = low_sum.astype(BF16)
    up_rows = up[adapter]
    low = low_sum.T.astype(BF16)
    for h in range(heads):
        part = slice(h * HEAD, (h + 1) * HEAD)
        q = rq[:, part].astype(F32) + dot(low, up_rows[:, part])
        qs[h * BLK : (h + 1) * BLK, :] = q.astype(BF16)

    u_rows = lax.broadcasted_iota(jnp.int32, (2 * BLK, CHUNK), 0)
    t_cols = lax.broadcasted_iota(jnp.int32, (2 * BLK, CHUNK), 1) % BLK

    def forward_unit(e, diagonal):
        low_edge = (first - 2 * (chip - e)) * BLK
        keys = kv[e, 0]
        values = kv[e, 1]
        values_t = values.T
        for ch in range(chunks):
            part = slice(ch * CHUNK, (ch + 1) * CHUNK)
            s = dot_nt(keys, qs[part, :])
            keep = u_rows >= low_edge
            if diagonal:
                keep = jnp.logical_and(keep, u_rows <= core * BLK + t_cols)
            s = jnp.where(keep, s, NEG)
            sbuf[e, :, part] = s
            dp = dot_nt(values, dos[part, :])
            dpbuf[e, :, part] = dp
            top = jnp.max(s, axis=0, keepdims=True)
            if not diagonal:
                was = stat[0:1, part]
                top = jnp.maximum(top, was)
            p = jnp.exp2(s * fold - top * fold)
            total = jnp.sum(p, axis=0, keepdims=True)
            delta = jnp.sum(p * dp, axis=0, keepdims=True)
            o = dot(values_t, p.astype(BF16))
            if not diagonal:
                shrink = jnp.exp2((was - top) * fold)
                total = total + shrink * stat[8:9, part]
                delta = delta + shrink * stat[16:17, part]
                o = o + shrink * ot[:, part]
            stat[0:1, part] = top
            stat[8:9, part] = total
            stat[16:17, part] = delta
            ot[:, part] = o

    forward_land(0).wait_recv()
    forward_unit(0, True)

    @pl.loop(1, earlier + 2)
    def _(e):
        @pl.when(e <= earlier)
        def _():
            kv_land(e).wait_recv()
            forward(e).start()

        @pl.when(e >= 2)
        def _():
            forward_land(e - 1).wait_recv()
            forward_unit(e - 1, False)

    total = stat[8:9, :]
    inverse = 1.0 / total
    stat[24:25, :] = stat[0:1, :] * fold + jnp.log(total) * LOG2E
    stat[16:17, :] = stat[16:17, :] * inverse
    for h in range(heads):
        part = slice(h * HEAD, (h + 1) * HEAD)
        outv[:, part] = (ot[:, part] * inverse[:, part]).T.astype(BF16)
    out_copy = pltpu.make_async_copy(outv, out_h, out_sem.at[0])
    out_copy.start()

    def sib_copy(e):
        return pltpu.make_async_remote_copy(
            src_ref=sib_out.at[e], dst_ref=sib_in.at[e],
            send_sem=sib_send.at[e], recv_sem=sib_recv.at[e],
            device_id=(sib, m), device_id_type=MESH,
        )

    def dkv_copy(e):
        return pltpu.make_async_remote_copy(
            src_ref=dkv_out.at[e], dst_ref=dkv_in.at[e],
            send_sem=dkv_send.at[e], recv_sem=dkv_recv.at[e],
            device_id=(own - 2 * e, m), device_id_type=MESH,
        )

    def dkv_land(e):
        return pltpu.make_async_remote_copy(
            src_ref=dkv_out.at[e], dst_ref=dkv_in.at[e],
            send_sem=dkv_send.at[e], recv_sem=dkv_recv.at[e],
            device_id=(sib, m), device_id_type=MESH,
        )

    dqt[...] = jnp.zeros_like(dqt)

    @pl.loop(0, earlier + 1)
    def _(turn):
        e = earlier - turn
        keys_t = kv[e, 0].T
        dk = jnp.zeros((2 * BLK, HEAD), F32)
        dv = jnp.zeros((2 * BLK, HEAD), F32)
        for ch in range(chunks):
            part = slice(ch * CHUNK, (ch + 1) * CHUNK)
            p = jnp.exp2(sbuf[e, :, part] * fold - stat[24:25, part])
            ds = (p * (dpbuf[e, :, part] - stat[16:17, part])).astype(BF16)
            dv = dv + dot(p.astype(BF16), dos[part, :])
            dk = dk + dot(ds, qs[part, :])
            dqt[:, part] = dqt[:, part] + dot(keys_t, ds)
        pair[0] = dk * scale
        pair[1] = dv
        own_st[e] = pair[:, mine, :]
        sib_out[e] = pair[:, other, :].astype(BF16)
        sib_copy(e).start()

        @pl.when(turn >= 1)
        def _():
            sib_copy(e + 1).wait_recv()
            dkv_out[e + 1] = (own_st[e + 1] + sib_in[e + 1].astype(F32)).astype(BF16)
            dkv_copy(e + 1).start()

    for h in range(heads):
        part = slice(h * HEAD, (h + 1) * HEAD)
        gqv[:, part] = (dqt[:, part] * scale).T.astype(BF16)
    dlowx[m] = dot_nt(up_rows, gqv[...])
    dlow_copies = exchange(dlowx, dlow_send, dlow_recv)
    for one in dlow_copies:
        one.start()
    gq_copy = pltpu.make_async_copy(gqv, gq_h, out_sem.at[1])
    gq_copy.start()

    half = seq // 2

    def a1_copy(index):
        return pltpu.make_async_remote_copy(
            src_ref=piece.at[index],
            dst_ref=got.at[pl.ds(pl.multiple_of(own * 8, 8), 8)],
            send_sem=a1_send, recv_sem=a1_recv,
            device_id=(index, m), device_id_type=MESH,
        )

    def spread(product, base):
        for t in range(cols // 128):
            for r in range(2):
                piece[base + t * 2 + r] = product[r * 8 : (r + 1) * 8, t * 128 : (t + 1) * 128]

        @pl.loop(0, half)
        def _(step):
            index = base + (own + step) % half

            @pl.when(index != own)
            def _():
                a1_copy(index).start()

    spread(dot(low_t, gqv[...]), 0)

    for one in dlow_copies:
        one.wait_recv()
    dlow_sum = dlowx[0]
    for step in range(1, mp):
        dlow_sum = dlow_sum + dlowx[step]
    spread(dot(dlow_sum.astype(BF16), hid[...]), half)
    mine8 = pl.ds(pl.multiple_of(own * 8, 8), 8)

    sib_copy(0).wait_recv()
    pair[:, 0:BLK, :] = own_st[0] + sib_in[0].astype(F32)

    @pl.loop(1, later + 1)
    def _(e):
        dkv_land(e).wait_recv()
        pair[:, 0:BLK, :] = pair[:, 0:BLK, :] + dkv_in[e].astype(F32)

    gkv[...] = pair[:, 0:BLK, :].astype(BF16)
    gk_copy = pltpu.make_async_copy(gkv.at[0], gk_h, out_sem.at[2])
    gv_copy = pltpu.make_async_copy(gkv.at[1], gv_h, out_sem.at[3])
    gk_copy.start()
    gv_copy.start()

    rest = (seq - 1) * 8
    pltpu.make_async_copy(got.at[pl.ds(0, rest)], got.at[pl.ds(0, rest)], a1_recv).wait()
    got[mine8, :] = piece[own]
    high = got[...].astype(BF16)
    tail = (got[...] - high.astype(F32)).astype(BF16)
    red[...] = dot(select[...], high) + dot(select[...], tail)

    @pl.loop(1, seq)
    def _(step):
        peer = (own + step) % seq
        pltpu.make_async_remote_copy(
            src_ref=red.at[pl.ds(pl.multiple_of(peer * 8, 8), 8)],
            dst_ref=fin.at[mine8],
            send_sem=a2_send, recv_sem=a2_recv,
            device_id=(peer, m), device_id_type=MESH,
        ).start()

    pltpu.make_async_copy(fin.at[pl.ds(0, rest)], fin.at[pl.ds(0, rest)], a2_recv).wait()
    fin[mine8, :] = red[mine8, :]
    for kind in range(2):
        for t in range(cols // 128):
            for r in range(2):
                at = (kind * half + t * 2 + r) * 8
                gout[kind, r * 8 : (r + 1) * 8, t * 128 : (t + 1) * 128] = fin[at : at + 8, :]
    gb_copy = pltpu.make_async_copy(gout.at[0], gb_h.at[0], out_sem.at[4])
    ga_copy = pltpu.make_async_copy(gout.at[1], ga_h.at[0], out_sem.at[5])
    gb_copy.start()
    ga_copy.start()

    for one in low_copies + dlow_copies:
        one.wait_send()

    @pl.loop(1, later + 1)
    def _(e):
        kv_copy(e).wait_send()

    @pl.loop(0, earlier + 1)
    def _(e):
        forward(e).wait_send()
        sib_copy(e).wait_send()

    @pl.loop(1, earlier + 1)
    def _(e):
        dkv_copy(e).wait_send()

    pltpu.make_async_copy(got.at[pl.ds(0, rest)], got.at[pl.ds(0, rest)], a1_send).wait()
    pltpu.make_async_copy(red.at[pl.ds(0, rest)], red.at[pl.ds(0, rest)], a2_send).wait()
    for one in (out_copy, gq_copy, gk_copy, gv_copy, ga_copy, gb_copy):
        one.wait()


def on_device(
    hidden_rows, rotated_queries, rotated_keys, value_rows, adapter_down, adapter_up,
    output_gradient, document_blocks, document_adapter,
):
    seq = lax.axis_size("seq")
    mp = lax.axis_size("mp")
    rows, cols = hidden_rows.shape
    adapters = adapter_down.shape[0]
    units = seq // 4 + 1
    any_space = pl.BlockSpec(memory_space=pl.ANY)
    smem = pl.BlockSpec(memory_space=pltpu.SMEM)
    dma = pltpu.SemaphoreType.DMA
    vmem = pltpu.VMEM
    return pl.pallas_call(
        functools.partial(kernel, seq, mp, document_blocks.shape[0]),
        out_shape=(
            jax.ShapeDtypeStruct((rows, cols), BF16),
            jax.ShapeDtypeStruct((rows, cols), BF16),
            jax.ShapeDtypeStruct((rows, HEAD), BF16),
            jax.ShapeDtypeStruct((rows, HEAD), BF16),
            jax.ShapeDtypeStruct((1, RANK, cols), F32),
            jax.ShapeDtypeStruct((1, RANK, cols), F32),
        ),
        in_specs=[smem, smem] + [any_space] * 7,
        out_specs=[any_space] * 6,
        scratch_shapes=[
            vmem((rows, cols), BF16),
            vmem((rows, cols), BF16),
            vmem((adapters, RANK, cols), BF16),
            vmem((adapters, RANK, cols), BF16),
            vmem((rows, cols), BF16),
            vmem((units, 2, 2 * BLK, HEAD), BF16),
            vmem((cols, HEAD), BF16),
            vmem((cols, HEAD), BF16),
            vmem((units, 2 * BLK, cols), F32),
            vmem((units, 2 * BLK, cols), F32),
            vmem((mp, RANK, rows), F32),
            vmem((mp, RANK, rows), F32),
            vmem((32, cols), F32),
            vmem((HEAD, cols), F32),
            vmem((HEAD, cols), F32),
            vmem((rows, cols), BF16),
            vmem((rows, cols), BF16),
            vmem((2, 2 * BLK, HEAD), F32),
            vmem((units, 2, BLK, HEAD), F32),
            vmem((units, 2, BLK, HEAD), BF16),
            vmem((units, 2, BLK, HEAD), BF16),
            vmem((units, 2, BLK, HEAD), BF16),
            vmem((units, 2, BLK, HEAD), BF16),
            vmem((2, BLK, HEAD), BF16),
            vmem((seq * 8, seq * 8), BF16),
            vmem((seq, 8, 128), F32),
            vmem((seq * 8, 128), F32),
            vmem((seq * 8, 128), F32),
            vmem((seq * 8, 128), F32),
            vmem((2, RANK, cols), F32),
            dma((7,)), dma((6,)),
            dma((mp,)), dma((mp,)), dma((mp,)), dma((mp,)),
            dma((units,)), dma((units,)), dma((units,)), dma((units,)),
            dma((units,)), dma((units,)), dma((units,)), dma((units,)),
            dma, dma, dma, dma,
        ],
        compiler_params=pltpu.CompilerParams(
            collective_id=0, has_side_effects=True, vmem_limit_bytes=48 * 1024 * 1024
        ),
    )(
        document_blocks, document_adapter, hidden_rows, rotated_queries, rotated_keys,
        value_rows, adapter_down, adapter_up, output_gradient,
    )


def solution(mesh):
    return jax.shard_map(
        on_device,
        mesh=mesh,
        in_specs=(
            P("seq", "mp"),
            P("seq", "mp"),
            P("seq", "mp"),
            P("seq", "mp"),
            P(None, None, "mp"),
            P(None, None, "mp"),
            P("seq", "mp"),
            P(),
            P(),
        ),
        out_specs=(
            P("seq", "mp"),
            P("seq", "mp"),
            P("seq", "mp"),
            P("seq", "mp"),
            P("seq", None, "mp"),
            P("seq", None, "mp"),
        ),
        check_vma=False,
    )
```

time: 377 us -> 64.9 us (0.17)
  waiting for transfers between devices: 216 us -> 0 us
  Pallas kernels: 0 us -> 51.8 us
  other arithmetic: 40.3 us -> 0 us
  between operations: 36.2 us -> 0.66 us
  blocking collectives: 31.8 us -> 0 us
  local copies, waits for them, and re-layouts: 32.5 us -> 12 us
  matrix products: 17.8 us -> 0 us
    reduce_scatter x2 -> x0, waiting for transfers between devices: 120 us -> none  [the longest x1 87.5 us: on_device(): lax.psum_scatter(terms_up.astype(jnp.bfloat16), 'seq', scatter_dimension=...]
    unnamed x5 -> x0, waiting for transfers between devices: 88.2 us -> none
    pallas_call x0 -> x1, Pallas kernels: none -> 51.8 us  [on_device(): pl.pallas_call(functools.partial(kernel, seq, mp, document_blocks.shape[0...]
    psum x2 -> x0, blocking collectives: 31.8 us -> none  [the longest x1 17.7 us: on_device(): low = lax.psum(low_part, 'mp').astype(jnp.bfloat16)]
    dynamic_update_slice x17 -> x0, other arithmetic: 26 us -> none  [on_device(): lax.dynamic_update_slice_in_dim(buffer, part + both[dist * rows:(dist + 1...]
    dot_general x11 -> x0, matrix products: 17.8 us -> none  [the longest x1 5.02 us: attend(): jnp.einsum('gjtu,tgjd->ugd', probs_b, grad_four, preferred_element_type=j...]
    unnamed x51 -> x24, local copies, waits for them, and re-layouts: 21.2 us -> 12 us
    all_gather x1 -> x0, waiting for transfers between devices: 7.23 us -> none  [on_device(): whole = lax.all_gather(kv_rows, 'seq', axis=0, tiled=True)]
  transfers between devices with their start and end apart: 4 -> 0, of which waited for: 4 -> 0; matrix products, arithmetic and copies ran while one was open for 16% -> 0% of each run, Pallas kernels for 0% -> 0%
where the time goes in v1:
time: 64.9 us; the launch traced here: 64.5 us
  Pallas kernels  51.8 us (80%)
  local copies, waits for them, and re-layouts  12 us (18%)
  between operations  0.66 us (1%)
    pallas_call x1, Pallas kernels, on_device(): pl.pallas_call(functools.partial(kernel, seq, mp, document_blocks.shape[0...  51.8 us
    unnamed x24, local copies, waits for them, and re-layouts  12 us

profile of v1, /device:TPU:1, one launch (start us, length us, event | category | flops | bytes accessed | tf_op | source)
XLA Modules:
  0.0 64.5 jit_solution(1847710028303897230)
XLA Ops:
  0.6 0.0 copy-start
  0.6 1.2 %copy-done = bf16[32,16,1024]{2,1,0:T(8,128)(2,1)S(1)} copy-done((bf16[32,16,1024]{2,1,0:T(8,128)(2,1)S(1)}, bf16[32,16,1024]{2,1,0:T(8,128)(2,1)}, u32[]{:S(2)}) %copy-start) | copy-done | bytes 1048600
  1.9 0.0 copy-start.1
  1.9 1.2 %copy-done.1 = bf16[32,16,1024]{2,1,0:T(8,128)(2,1)S(1)} copy-done((bf16[32,16,1024]{2,1,0:T(8,128)(2,1)S(1)}, bf16[32,16,1024]{2,1,0:T(8,128)(2,1)}, u32[]{:S(2)}) %copy-start.1) | copy-done | bytes 1048600
  3.1 0.0 copy-start.2
  3.1 0.9 %copy-done.2 = bf16[128,1024]{1,0:T(8,128)(2,1)S(1)} copy-done((bf16[128,1024]{1,0:T(8,128)(2,1)S(1)}, bf16[128,1024]{1,0:T(8,128)(2,1)}, u32[]{:S(2)}) %copy-start.2) | copy-done | bytes 262168
  4.0 0.0 copy-start.3
  4.0 0.9 %copy-done.3 = bf16[128,1024]{1,0:T(8,128)(2,1)S(1)} copy-done((bf16[128,1024]{1,0:T(8,128)(2,1)S(1)}, bf16[128,1024]{1,0:T(8,128)(2,1)}, u32[]{:S(2)}) %copy-start.3) | copy-done | bytes 262168
  5.0 0.0 copy-start.4
  5.0 0.9 %copy-done.4 = bf16[128,1024]{1,0:T(8,128)(2,1)S(1)} copy-done((bf16[128,1024]{1,0:T(8,128)(2,1)S(1)}, bf16[128,1024]{1,0:T(8,128)(2,1)}, u32[]{:S(2)}) %copy-start.4) | copy-done | bytes 262168
  5.9 0.0 copy-start.5
  5.9 0.8 %copy-done.5 = bf16[128,128]{1,0:T(8,128)(2,1)S(1)} copy-done((bf16[128,128]{1,0:T(8,128)(2,1)S(1)}, bf16[128,128]{1,0:T(8,128)(2,1)}, u32[]{:S(2)}) %copy-start.5) | copy-done | bytes 32792
  6.7 0.0 copy-start.6
  6.7 0.8 %copy-done.6 = bf16[128,128]{1,0:T(8,128)(2,1)S(1)} copy-done((bf16[128,128]{1,0:T(8,128)(2,1)S(1)}, bf16[128,128]{1,0:T(8,128)(2,1)}, u32[]{:S(2)}) %copy-start.6) | copy-done | bytes 32792
  7.5 0.0 copy-start.7
  7.5 0.7 %copy-done.7 = s32[9]{0:T(128)S(1)} copy-done((s32[9]{0:T(128)S(1)}, s32[9]{0:T(128)}, u32[]{:S(2)}) %copy-start.7) | copy-done | bytes 60
  8.1 0.0 copy-start.8
  8.1 0.7 %copy-done.8 = s32[9]{0:T(128)S(1)} copy-done((s32[9]{0:T(128)S(1)}, s32[9]{0:T(128)}, u32[]{:S(2)}) %copy-start.8) | copy-done | bytes 60
  8.8 51.8 %shard_map.136 = (bf16[128,1024]{1,0:T(8,128)(2,1)S(1)}, bf16[128,1024]{1,0:T(8,128)(2,1)S(1)}, bf16[128,128]{1,0:T(8,128)(2,1)S(1)}, bf16[128,128]{1,0:T(8,128)...) custom-call(s32[9]{0:T(128)S(1)} %copy-done.7, s32[9]{0:T(128)S(1)} %copy-done.8, ...), custom_call_target="tpu_custom_call" | custom-call | tf_op jit(solution)/shard_map/pallas_call | solution.py:425
  60.6 0.7 %copy.21 = bf16[128,1024]{1,0:T(8,128)(2,1)} copy(bf16[128,1024]{1,0:T(8,128)(2,1)S(1)} %get-tuple-element.12) | data formatting | bytes 524288
  61.3 0.7 %copy.22 = bf16[128,1024]{1,0:T(8,128)(2,1)} copy(bf16[128,1024]{1,0:T(8,128)(2,1)S(1)} %get-tuple-element.13) | data formatting | bytes 524288
  62.0 0.6 copy.23
  62.6 0.6 copy.24
  63.2 0.6 copy.25
  63.9 0.6 copy.26
Async XLA Ops:
  0.6 1.2 %copy-start = (bf16[32,16,1024]{2,1,0:T(8,128)(2,1)S(1)}, bf16[32,16,1024]{2,1,0:T(8,128)(2,1)}, u32[]{:S(2)}) copy-start(bf16[32,16,1024]{2,1,0:T(8,128)(2,1)} %down_h.1) | copy-start | bytes 3145732
  1.9 1.2 %copy-start.1 = (bf16[32,16,1024]{2,1,0:T(8,128)(2,1)S(1)}, bf16[32,16,1024]{2,1,0:T(8,128)(2,1)}, u32[]{:S(2)}) copy-start(bf16[32,16,1024]{2,1,0:T(8,128)(2,1)} %up_h.1) | copy-start | bytes 3145732
  3.1 0.9 %copy-start.2 = (bf16[128,1024]{1,0:T(8,128)(2,1)S(1)}, bf16[128,1024]{1,0:T(8,128)(2,1)}, u32[]{:S(2)}) copy-start(bf16[128,1024]{1,0:T(8,128)(2,1)} %hid_h.1) | copy-start | bytes 786436
  4.0 0.9 %copy-start.3 = (bf16[128,1024]{1,0:T(8,128)(2,1)S(1)}, bf16[128,1024]{1,0:T(8,128)(2,1)}, u32[]{:S(2)}) copy-start(bf16[128,1024]{1,0:T(8,128)(2,1)} %rq_h.1) | copy-start | bytes 786436
  5.0 0.9 %copy-start.4 = (bf16[128,1024]{1,0:T(8,128)(2,1)S(1)}, bf16[128,1024]{1,0:T(8,128)(2,1)}, u32[]{:S(2)}) copy-start(bf16[128,1024]{1,0:T(8,128)(2,1)} %do_h.1) | copy-start | bytes 786436
  5.9 0.8 %copy-start.5 = (bf16[128,128]{1,0:T(8,128)(2,1)S(1)}, bf16[128,128]{1,0:T(8,128)(2,1)}, u32[]{:S(2)}) copy-start(bf16[128,128]{1,0:T(8,128)(2,1)} %k_h.1) | copy-start | bytes 98308
  6.7 0.8 %copy-start.6 = (bf16[128,128]{1,0:T(8,128)(2,1)S(1)}, bf16[128,128]{1,0:T(8,128)(2,1)}, u32[]{:S(2)}) copy-start(bf16[128,128]{1,0:T(8,128)(2,1)} %v_h.1) | copy-start | bytes 98308
  7.5 0.7 %copy-start.7 = (s32[9]{0:T(128)S(1)}, s32[9]{0:T(128)}, u32[]{:S(2)}) copy-start(s32[9]{0:T(128)} %db.1) | copy-start | bytes 112
  8.1 0.7 %copy-start.8 = (s32[9]{0:T(128)S(1)}, s32[9]{0:T(128)}, u32[]{:S(2)}) copy-start(s32[9]{0:T(128)} %da.1) | copy-start | bytes 112

commit v2 on v1

v2 whole, which is shorter than its diff:
```python
import functools
import math

import jax
import jax.numpy as jnp
from jax import lax
from jax.experimental import pallas as pl
from jax.experimental.pallas import tpu as pltpu
from jax.sharding import PartitionSpec as P

HEAD = 128
BLK = 128
RANK = 16
CHUNK = 1024
NARROW = 256
GROUP = 3
LAG = 3
NEG = -1e30
LOG2E = 1.4426950408889634
MESH = pl.DeviceIdType.MESH
F32 = jnp.float32
BF16 = jnp.bfloat16

NT = (((1,), (1,)), ((), ()))


def dot(a, b):
    return jnp.dot(a, b, preferred_element_type=F32)


def dot_nt(a, b):
    return lax.dot_general(a, b, NT, preferred_element_type=F32)


def kernel(
    seq, mp, docs,
    db_h, da_h, hid_h, rq_h, k_h, v_h, down_h, up_h, do_h,
    out_h, gq_h, gk_h, gv_h, ga_h, gb_h,
    db, da, hid, rq, down, up, do, kv, qs, qt, dos, dot_t, sbuf, dpbuf, pbuf, dsbuf,
    lowx, dlowx, stat, keys_t, vals_t, outv, gqv, pair, own_st, sib_out, sib_in,
    dkv_out, dkv_in, home_out, home_in, gkv, total_kv, select, piece, got, red, fin, gout,
    load_sem, out_sem,
    low_send, low_recv, dlow_send, dlow_recv,
    col_send, row_send, kv_recv, fwd_send, fwd_recv, sib_send, sib_recv, dkv_send, dkv_recv,
    home_send, home_recv,
    a1_send, a1_recv, a2_send, a2_recv,
):
    reach = seq // 4
    chips = seq // 2
    units = reach + 1
    wide = reach // 2
    tall = chips // wide
    cols = hid.shape[1]
    heads = cols // HEAD
    span = cols // 128
    groups = units // GROUP
    scale = 1.0 / math.sqrt(HEAD)
    fold = scale * LOG2E

    own = lax.axis_index("seq")
    m = lax.axis_index("mp")
    chip = own // 2
    core = own % 2
    sib = own + 1 - 2 * core
    place = own % span
    base = own - place
    mine = pl.ds(pl.multiple_of(core * BLK, BLK), BLK)
    other = pl.ds(pl.multiple_of((1 - core) * BLK, BLK), BLK)
    x = chip % wide
    y = chip // wide
    earlier = jnp.minimum(reach, chip)

    def load(src, dst, n):
        return pltpu.make_async_copy(src, dst, load_sem.at[n])

    loads = [
        load(k_h, kv.at[0, 0, mine], 0),
        load(v_h, kv.at[0, 1, mine], 1),
        load(hid_h, hid, 2),
        load(down_h, down, 3),
        load(up_h, up, 4),
        load(rq_h, rq, 5),
        load(do_h, do, 6),
        load(db_h, db, 7),
        load(da_h, da, 8),
    ]
    loads[0].start()
    loads[1].start()
    barrier = pltpu.get_barrier_semaphore()
    partners = [(own, (m + step) % mp) for step in range(1, mp)]
    partners += [(base + (place + step) % span, m) for step in range(1, span)]
    partners += [((own + span * step) % seq, m) for step in range(1, seq // span)]
    for peer in partners:
        pl.semaphore_signal(barrier, inc=1, device_id=peer, device_id_type=MESH)
    for n in (7, 8, 2, 3, 6, 4, 5):
        loads[n].start()
    loads[0].wait()
    loads[1].wait()
    pl.semaphore_wait(barrier, len(partners))

    def exchange(buf, send, recv):
        copies = []
        for step in range(1, mp):
            peer = (m + step) % mp
            copies.append(
                pltpu.make_async_remote_copy(
                    src_ref=buf.at[m], dst_ref=buf.at[m],
                    send_sem=send.at[step], recv_sem=recv.at[step],
                    device_id=(own, peer), device_id_type=MESH,
                )
            )
        return copies

    def at_chip(to_x, to_y):
        return ((to_y * wide + to_x) * 2 + core, m)

    def column_copy(dy):
        return pltpu.make_async_remote_copy(
            src_ref=kv.at[0, :, mine], dst_ref=kv.at[dy * wide, :, mine],
            send_sem=col_send.at[dy], recv_sem=kv_recv.at[dy * wide],
            device_id=at_chip(x, y + dy), device_id_type=MESH,
        )

    def row_copy(dy, to_x):
        return pltpu.make_async_remote_copy(
            src_ref=kv.at[dy * wide, :, mine], dst_ref=kv.at[dy * wide + to_x - x, :, mine],
            send_sem=row_send.at[dy, to_x], recv_sem=kv_recv.at[dy * wide + to_x - x],
            device_id=at_chip(to_x, y), device_id_type=MESH,
        )

    def row_readers(dy, act):
        for to_x in range(wide):
            reads = (to_x > x, to_x != x, to_x < x)[dy]

            @pl.when(jnp.logical_and(y >= dy, reads))
            def _():
                act(row_copy(dy, to_x))

    def kv_land(e):
        return pltpu.make_async_remote_copy(
            src_ref=kv.at[0, :, mine], dst_ref=kv.at[e, :, mine],
            send_sem=col_send.at[0], recv_sem=kv_recv.at[e],
            device_id=(sib, m), device_id_type=MESH,
        )

    def forward(e):
        return pltpu.make_async_remote_copy(
            src_ref=kv.at[e, :, mine], dst_ref=kv.at[e, :, mine],
            send_sem=fwd_send.at[e], recv_sem=fwd_recv.at[e],
            device_id=(sib, m), device_id_type=MESH,
        )

    def forward_land(e):
        return pltpu.make_async_remote_copy(
            src_ref=kv.at[e, :, other], dst_ref=kv.at[e, :, other],
            send_sem=fwd_send.at[e], recv_sem=fwd_recv.at[e],
            device_id=(sib, m), device_id_type=MESH,
        )

    @pl.when(y + 1 < tall)
    def _():
        column_copy(1).start()

    forward(0).start()
    row_readers(0, lambda copy: copy.start())

    loads[7].wait()
    loads[8].wait()
    start = jnp.int32(0)
    first = jnp.int32(0)
    adapter = jnp.int32(0)
    bounds = []
    for d in range(docs):
        end = start + db[d]
        inside = jnp.logical_and(own >= start, own < end)
        first = jnp.where(inside, start, first)
        adapter = jnp.where(inside, da[d], adapter)
        bounds.append((start, end, da[d]))
        start = end

    loads[2].wait()
    loads[3].wait()
    lowx[m] = dot_nt(down[adapter], hid[...])
    low_copies = exchange(lowx, low_send, low_recv)
    for one in low_copies:
        one.start()

    @pl.when(y + 1 < tall)
    def _():
        column_copy(1).wait_send()

    @pl.when(y + 2 < tall)
    def _():
        column_copy(2).start()

    loads[6].wait()
    for h in range(heads):
        here = slice(h * BLK, (h + 1) * BLK)
        part = do[:, h * HEAD : (h + 1) * HEAD]
        dos[here, :] = part
        dot_t[:, here] = part.T

    size = select.shape
    row = lax.broadcasted_iota(jnp.int32, size, 0)
    col = lax.broadcasted_iota(jnp.int32, size, 1)
    same = (row % RANK) == (col % RANK)
    row_a = row // RANK
    col_s = base + col // RANK
    hit = jnp.zeros(size, F32)
    for begin, end, name in bounds:
        inside = jnp.logical_and(col_s >= begin, col_s < end)
        inside = jnp.logical_and(inside, row_a == name)
        hit = jnp.where(jnp.logical_and(inside, same), 1.0, hit)
    select[...] = hit.astype(BF16)

    @pl.loop(earlier + 1, units)
    def _(e):
        sbuf[e] = jnp.full(sbuf.shape[1:], NEG, F32)
        dpbuf[e] = jnp.zeros(dpbuf.shape[1:], F32)
        kv[e] = jnp.zeros(kv.shape[1:], BF16)

    for dy in range(1, 3):

        @pl.when(y >= dy)
        def _():
            kv_land(dy * wide).wait_recv()
            forward(dy * wide).start()

        row_readers(dy, lambda copy: copy.start())

    @pl.loop(1, x + 1)
    def _(e):
        kv_land(e).wait_recv()
        forward(e).start()

    loads[4].wait()
    loads[5].wait()
    up_rows = up[adapter]
    for one in low_copies:
        one.wait_recv()
    low_sum = lowx[0]
    for step in range(1, mp):
        low_sum = low_sum + lowx[step]
    low_t = low_sum.astype(BF16)
    low = low_sum.T.astype(BF16)
    for h in range(heads):
        part = slice(h * HEAD, (h + 1) * HEAD)
        here = slice(h * BLK, (h + 1) * BLK)
        q = (rq[:, part].astype(F32) + dot(low, up_rows[:, part])).astype(BF16)
        qs[here, :] = q
        qt[:, here] = q.T

    u_rows = lax.broadcasted_iota(jnp.int32, (2 * BLK, CHUNK), 0)
    t_cols = lax.broadcasted_iota(jnp.int32, (2 * BLK, CHUNK), 1) % BLK

    def score_unit(e, diagonal):
        low_edge = (first - 2 * (chip - e)) * BLK
        keys = kv[e, 0]
        values = kv[e, 1]
        for at in range(0, cols, CHUNK):
            part = slice(at, at + CHUNK)
            s = dot(keys, qt[:, part])
            keep = u_rows >= low_edge
            if diagonal:
                keep = jnp.logical_and(keep, u_rows <= core * BLK + t_cols)
            s = jnp.where(keep, s, NEG)
            sbuf[e, :, part] = s
            dp = dot(values, dot_t[:, part])
            dpbuf[e, :, part] = dp
            top = jnp.max(s, axis=0, keepdims=True)
            if not diagonal:
                was = stat[0:1, part]
                top = jnp.maximum(top, was)
            p = jnp.exp2(s * fold - top * fold)
            total = jnp.sum(p, axis=0, keepdims=True)
            delta = jnp.sum(p * dp, axis=0, keepdims=True)
            if not diagonal:
                shrink = jnp.exp2((was - top) * fold)
                total = total + shrink * stat[8:9, part]
                delta = delta + shrink * stat[16:17, part]
            stat[0:1, part] = top
            stat[8:9, part] = total
            stat[16:17, part] = delta

    forward_land(0).wait_recv()
    score_unit(0, True)

    for dy in range(1, 3):

        @pl.when(y >= dy)
        def _():
            forward_land(dy * wide).wait_recv()
            score_unit(dy * wide, False)

    @pl.loop(1, earlier + 1 + LAG)
    def _(e):
        @pl.when(jnp.logical_and(jnp.logical_and(e > x, e <= earlier), e % wide != 0))
        def _():
            kv_land(e).wait_recv()
            forward(e).start()

        @pl.when(jnp.logical_and(e > LAG, (e - LAG) % wide != 0))
        def _():
            forward_land(e - LAG).wait_recv()
            score_unit(e - LAG, False)

    total = stat[8:9, :]
    stat[24:25, :] = stat[0:1, :] * fold + jnp.log(total) * LOG2E
    stat[16:17, :] = stat[16:17, :] / total
    for e in range(units):
        here = slice(e * 2 * BLK, (e + 1) * 2 * BLK)
        keys_t[:, here] = kv[e, 0].T
        vals_t[:, here] = kv[e, 1].T
        for at in range(0, cols, NARROW):
            part = slice(at, at + NARROW)
            p = jnp.exp2(sbuf[e, :, part] * fold - stat[24:25, part])
            dsbuf[here, part] = (p * (dpbuf[e, :, part] - stat[16:17, part])).astype(BF16)
            pbuf[here, part] = p.astype(BF16)
    dq_t = dot(keys_t[...], dsbuf[...]) * scale
    for h in range(heads):
        part = slice(h * HEAD, (h + 1) * HEAD)
        gqv[:, part] = dq_t[:, part].T.astype(BF16)

    dlowx[m] = dot_nt(up_rows, gqv[...])
    dlow_copies = exchange(dlowx, dlow_send, dlow_recv)
    for one in dlow_copies:
        one.start()
    gq_copy = pltpu.make_async_copy(gqv, gq_h, out_sem.at[1])
    gq_copy.start()

    own16 = pl.ds(pl.multiple_of(own * RANK, RANK), RANK)
    place16 = pl.ds(pl.multiple_of(place * RANK, RANK), RANK)
    rest1 = pl.ds(0, (span - 1) * RANK)
    rest2 = pl.ds(0, (seq - 1) * RANK)

    def spread(kind, product):
        for t in range(span):
            piece[kind, t] = product[:, t * 128 : (t + 1) * 128].astype(BF16)

        @pl.loop(1, span)
        def _(step):
            peer = (place + step) % span
            pltpu.make_async_remote_copy(
                src_ref=piece.at[kind, peer], dst_ref=got.at[kind, place16],
                send_sem=a1_send.at[kind], recv_sem=a1_recv.at[kind],
                device_id=(base + peer, m), device_id_type=MESH,
            ).start()

    def settle(kind):
        land = got.at[kind, rest1]
        pltpu.make_async_copy(land, land, a1_recv.at[kind]).wait()
        got[kind, place16, :] = piece[kind, place]
        red[kind] = dot(select[...], got[kind]).astype(BF16)

        @pl.loop(1, seq)
        def _(step):
            peer = (own + step) % seq
            pltpu.make_async_remote_copy(
                src_ref=red.at[kind, pl.ds(pl.multiple_of(peer * RANK, RANK), RANK)],
                dst_ref=fin.at[kind, own16],
                send_sem=a2_send.at[kind], recv_sem=a2_recv.at[kind],
                device_id=(peer, m), device_id_type=MESH,
            ).start()

    def finish(kind):
        land = fin.at[kind, rest2]
        pltpu.make_async_copy(land, land, a2_recv.at[kind]).wait()
        fin[kind, own16, :] = red[kind, own16, :]
        for t in range(span):
            whole = jnp.zeros((RANK, 128), F32)
            for line in range(seq // span):
                at = (line * span + t) * RANK
                whole = whole + fin[kind, at : at + RANK, :].astype(F32)
            gout[kind, :, t * 128 : (t + 1) * 128] = whole

    def sib_copy(g):
        return pltpu.make_async_remote_copy(
            src_ref=sib_out.at[g], dst_ref=sib_in.at[g],
            send_sem=sib_send.at[g], recv_sem=sib_recv.at[g],
            device_id=(sib, m), device_id_type=MESH,
        )

    def merge_copy(e):
        owner = chip - e
        to_x = owner % wide
        dy = y - owner // wide
        return to_x, pltpu.make_async_remote_copy(
            src_ref=dkv_out.at[e], dst_ref=dkv_in.at[dy, x],
            send_sem=dkv_send.at[e], recv_sem=dkv_recv.at[dy, x],
            device_id=at_chip(to_x, y), device_id_type=MESH,
        )

    def merge_land(dy, from_x):
        return pltpu.make_async_remote_copy(
            src_ref=dkv_out.at[0], dst_ref=dkv_in.at[dy, from_x],
            send_sem=dkv_send.at[0], recv_sem=dkv_recv.at[dy, from_x],
            device_id=(sib, m), device_id_type=MESH,
        )

    def home_copy(dy):
        return pltpu.make_async_remote_copy(
            src_ref=home_out.at[dy], dst_ref=home_in.at[dy],
            send_sem=home_send.at[dy], recv_sem=home_recv.at[dy],
            device_id=at_chip(x, y - dy), device_id_type=MESH,
        )

    def merge_row(dy):
        for from_x in range(wide):
            writes = (from_x > x, from_x != x, from_x < x)[dy]

            @pl.when(jnp.logical_and(y >= dy, writes))
            def _():
                merge_land(dy, from_x).wait_recv()
                total_kv[dy] = total_kv[dy] + dkv_in[dy, from_x].astype(F32)

    def weigh(g):
        here = slice(g * GROUP * 2 * BLK, (g + 1) * GROUP * 2 * BLK)
        pair[0] = dot(dsbuf[here, :], qs[...]) * scale
        pair[1] = dot(pbuf[here, :], dos[...])
        for k in range(GROUP):
            for kind in range(2):
                lower = pl.ds(pl.multiple_of((2 * k + core) * BLK, BLK), BLK)
                upper = pl.ds(pl.multiple_of((2 * k + 1 - core) * BLK, BLK), BLK)
                own_st[g, k, kind] = pair[kind, lower, :]
                sib_out[g, k, kind] = pair[kind, upper, :].astype(BF16)
        sib_copy(g).start()

    def pass_on(g):
        sib_copy(g).wait_recv()
        for k in range(GROUP - 1, -1, -1):
            e = g * GROUP + k
            merged = own_st[g, k] + sib_in[g, k].astype(F32)
            if e % wide == 0:
                total_kv[e // wide] = merged
            else:
                dkv_out[e] = merged.astype(BF16)
                to_x, copy = merge_copy(e)

                @pl.when(e <= earlier)
                def _():
                    copy.start()

    spread(0, dot(low_t, gqv[...]))
    for g in range(groups - 1, -1, -1):
        weigh(g)
        if g < groups - 1:
            pass_on(g + 1)

    for one in dlow_copies:
        one.wait_recv()
    dlow_sum = dlowx[0]
    for step in range(1, mp):
        dlow_sum = dlow_sum + dlowx[step]
    spread(1, dot(dlow_sum.astype(BF16), hid[...]))
    pass_on(0)
    settle(0)

    out_t = dot(vals_t[...], pbuf[...])
    for h in range(heads):
        part = slice(h * HEAD, (h + 1) * HEAD)
        outv[:, part] = out_t[:, part].T.astype(BF16)
    out_copy = pltpu.make_async_copy(outv, out_h, out_sem.at[0])
    out_copy.start()

    def send_home(dy):
        merge_row(dy)

        @pl.when(y >= dy)
        def _():
            home_out[dy] = total_kv[dy].astype(BF16)
            home_copy(dy).start()

    send_home(2)
    settle(1)
    send_home(1)
    merge_row(0)
    finish(0)
    gb_copy = pltpu.make_async_copy(gout.at[0], gb_h.at[0], out_sem.at[4])
    gb_copy.start()
    for dy in range(1, 3):

        @pl.when(y + dy < tall)
        def _():
            home_copy(dy).wait_recv()
            total_kv[0] = total_kv[0] + home_in[dy].astype(F32)

    gkv[...] = total_kv[0].astype(BF16)
    gk_copy = pltpu.make_async_copy(gkv.at[0], gk_h, out_sem.at[2])
    gv_copy = pltpu.make_async_copy(gkv.at[1], gv_h, out_sem.at[3])
    gk_copy.start()
    gv_copy.start()

    finish(1)
    ga_copy = pltpu.make_async_copy(gout.at[1], ga_h.at[0], out_sem.at[5])
    ga_copy.start()

    for one in low_copies + dlow_copies:
        one.wait_send()

    for dy in range(3):
        row_readers(dy, lambda copy: copy.wait_send())
    for dy in range(1, 3):

        @pl.when(y >= dy)
        def _():
            home_copy(dy).wait_send()

    @pl.when(y + 2 < tall)
    def _():
        column_copy(2).wait_send()

    @pl.loop(0, earlier + 1)
    def _(e):
        forward(e).wait_send()

    for g in range(groups):
        sib_copy(g).wait_send()
    for e in range(units):
        if e % wide:
            to_x, copy = merge_copy(e)

            @pl.when(e <= earlier)
            def _():
                copy.wait_send()

    for kind in range(2):
        sent = got.at[kind, rest1]
        pltpu.make_async_copy(sent, sent, a1_send.at[kind]).wait()
        sent = red.at[kind, rest2]
        pltpu.make_async_copy(sent, sent, a2_send.at[kind]).wait()
    for one in (out_copy, gq_copy, gk_copy, gv_copy, ga_copy, gb_copy):
        one.wait()


def place_kernel(count, *refs):
    sources, targets, held = refs[:count], refs[count : 2 * count], refs[2 * count : 3 * count]
    in_sem, out_sem = refs[3 * count :]
    ins = [pltpu.make_async_copy(sources[n], held[n], in_sem.at[n]) for n in range(count)]
    outs = [pltpu.make_async_copy(held[n], targets[n], out_sem.at[n]) for n in range(count)]
    for one in ins:
        one.start()
    for came, goes in zip(ins, outs):
        came.wait()
        goes.start()
    for one in outs:
        one.wait()


def on_device(
    hidden_rows, rotated_queries, rotated_keys, value_rows, adapter_down, adapter_up,
    output_gradient, document_blocks, document_adapter,
):
    seq = lax.axis_size("seq")
    mp = lax.axis_size("mp")
    rows, cols = hidden_rows.shape
    adapters = adapter_down.shape[0]
    units = seq // 4 + 1
    wide = seq // 8
    span = cols // 128
    groups = units // GROUP
    docs = document_blocks.shape[0]
    any_space = pl.BlockSpec(memory_space=pl.ANY)
    dma = pltpu.SemaphoreType.DMA
    vmem = pltpu.VMEM
    shapes = (
        jax.ShapeDtypeStruct((rows, cols), BF16),
        jax.ShapeDtypeStruct((rows, cols), BF16),
        jax.ShapeDtypeStruct((rows, HEAD), BF16),
        jax.ShapeDtypeStruct((rows, HEAD), BF16),
        jax.ShapeDtypeStruct((1, RANK, cols), F32),
        jax.ShapeDtypeStruct((1, RANK, cols), F32),
    )
    made = pl.pallas_call(
        functools.partial(kernel, seq, mp, docs),
        out_shape=shapes,
        in_specs=[any_space] * 9,
        out_specs=[any_space] * 6,
        scratch_shapes=[
            pltpu.SMEM((docs,), jnp.int32),
            pltpu.SMEM((docs,), jnp.int32),
            vmem((rows, cols), BF16),
            vmem((rows, cols), BF16),
            vmem((adapters, RANK, cols), BF16),
            vmem((adapters, RANK, cols), BF16),
            vmem((rows, cols), BF16),
            vmem((units, 2, 2 * BLK, HEAD), BF16),
            vmem((cols, HEAD), BF16),
            vmem((HEAD, cols), BF16),
            vmem((cols, HEAD), BF16),
            vmem((HEAD, cols), BF16),
            vmem((units, 2 * BLK, cols), F32),
            vmem((units, 2 * BLK, cols), F32),
            vmem((units * 2 * BLK, cols), BF16),
            vmem((units * 2 * BLK, cols), BF16),
            vmem((mp, RANK, rows), F32),
            vmem((mp, RANK, rows), F32),
            vmem((32, cols), F32),
            vmem((HEAD, units * 2 * BLK), BF16),
            vmem((HEAD, units * 2 * BLK), BF16),
            vmem((rows, cols), BF16),
            vmem((rows, cols), BF16),
            vmem((2, GROUP * 2 * BLK, HEAD), F32),
            vmem((groups, GROUP, 2, BLK, HEAD), F32),
            vmem((groups, GROUP, 2, BLK, HEAD), BF16),
            vmem((groups, GROUP, 2, BLK, HEAD), BF16),
            vmem((units, 2, BLK, HEAD), BF16),
            vmem((3, wide, 2, BLK, HEAD), BF16),
            vmem((3, 2, BLK, HEAD), BF16),
            vmem((3, 2, BLK, HEAD), BF16),
            vmem((2, BLK, HEAD), BF16),
            vmem((3, 2, BLK, HEAD), F32),
            vmem((adapters * RANK, span * RANK), BF16),
            vmem((2, span, RANK, 128), BF16),
            vmem((2, span * RANK, 128), BF16),
            vmem((2, seq * RANK, 128), BF16),
            vmem((2, seq * RANK, 128), BF16),
            vmem((2, RANK, cols), F32),
            dma((9,)), dma((6,)),
            dma((mp,)), dma((mp,)), dma((mp,)), dma((mp,)),
            dma((3,)), dma((3, wide)), dma((units,)), dma((units,)), dma((units,)),
            dma((groups,)), dma((groups,)), dma((units,)), dma((3, wide)),
            dma((3,)), dma((3,)),
            dma((2,)), dma((2,)), dma((2,)), dma((2,)),
        ],
        compiler_params=pltpu.CompilerParams(
            collective_id=0, has_side_effects=True, vmem_limit_bytes=63 * 1024 * 1024
        ),
    )(
        document_blocks, document_adapter, hidden_rows, rotated_queries, rotated_keys,
        value_rows, adapter_down, adapter_up, output_gradient,
    )
    return pl.pallas_call(
        functools.partial(place_kernel, len(shapes)),
        out_shape=shapes,
        in_specs=[any_space] * len(shapes),
        out_specs=[any_space] * len(shapes),
        scratch_shapes=[vmem(one.shape, one.dtype) for one in shapes]
        + [dma((len(shapes),)), dma((len(shapes),))],
    )(*made)


def solution(mesh):
    return jax.shard_map(
        on_device,
        mesh=mesh,
        in_specs=(
            P("seq", "mp"),
            P("seq", "mp"),
            P("seq", "mp"),
            P("seq", "mp"),
            P(None, None, "mp"),
            P(None, None, "mp"),
            P("seq", "mp"),
            P(),
            P(),
        ),
        out_specs=(
            P("seq", "mp"),
            P("seq", "mp"),
            P("seq", "mp"),
            P("seq", "mp"),
            P("seq", None, "mp"),
            P("seq", None, "mp"),
        ),
        check_vma=False,
    )
```

time: 64.9 us -> 47.6 us (0.73)
  local copies, waits for them, and re-layouts: 12 us -> 0 us
  Pallas kernels: 51.8 us -> 46.8 us
    unnamed x24 -> x0, local copies, waits for them, and re-layouts: 12 us -> none
    pallas_call x1 -> x2, Pallas kernels: 51.8 us -> 46.8 us  [the longest x1 44.9 us: on_device(): pl.pallas_call(functools.partial(kernel, seq, mp, docs), out_shape=shapes...]
where the time goes in v2:
time: 47.6 us; the launch traced here: 47.4 us
  Pallas kernels  46.8 us (98%)
  between operations  0.64 us (1%)
    pallas_call x1, Pallas kernels, on_device(): pl.pallas_call(functools.partial(kernel, seq, mp, docs), out_shape=shapes...  44.9 us
    pallas_call x1, Pallas kernels, on_device(): pl.pallas_call(functools.partial(place_kernel, len(shapes)), out_shape=sh...  1.9 us

profile of v2, /device:TPU:1, one launch (start us, length us, event | category | flops | bytes accessed | tf_op | source)
XLA Modules:
  0.0 47.4 jit_solution(3513564082265656270)
XLA Ops:
  0.6 44.9 %shard_map.136 = (bf16[128,1024]{1,0:T(8,128)(2,1)}, bf16[128,1024]{1,0:T(8,128)(2,1)}, bf16[128,128]{1,0:T(8,128)(2,1)}, bf16[128,128]{1,0:T(8,128)(2,1)}, f32[...) custom-call(s32[9]{0:T(128)} %db_h.1, s32[9]{0:T(128)} %da_h.1, bf16[128,1024]{1,0:T(8,128)(2,1)} %hid_h.1, ...), custom_call_target="tpu_custom_call" | custom-call | tf_op jit(solution)/shard_map/pallas_call | solution.py:573
  45.5 1.9 %shard_map.137 = (bf16[128,1024]{1,0:T(8,128)(2,1)}, bf16[128,1024]{1,0:T(8,128)(2,1)}, bf16[128,128]{1,0:T(8,128)(2,1)}, bf16[128,128]{1,0:T(8,128)(2,1)}, f32[...) custom-call(bf16[128,1024]{1,0:T(8,128)(2,1)} %get-tuple-element.12.refs_0_, bf16[128,1024]{1,0:T(8,128)(2,1)} %get-tuple-element.13.refs_1_, ...), custom_call_target="tpu_custom_call" | custom-call | tf_op jit(solution)/shard_map/pallas_call | solution.py:632

commit v3 on v2

--- a/solution.py
+++ b/solution.py
@@ -35,13 +35,13 @@
 def kernel(
     seq, mp, docs,
     db_h, da_h, hid_h, rq_h, k_h, v_h, down_h, up_h, do_h,
-    out_h, gq_h, gk_h, gv_h, ga_h, gb_h,
+    outv, gqv, gk, gv, ga, gb,
     db, da, hid, rq, down, up, do, kv, qs, qt, dos, dot_t, sbuf, dpbuf, pbuf, dsbuf,
-    lowx, dlowx, stat, keys_t, vals_t, outv, gqv, pair, own_st, sib_out, sib_in,
-    dkv_out, dkv_in, home_out, home_in, gkv, total_kv, select, piece, got, red, fin, gout,
-    load_sem, out_sem,
+    lowx, dlowx, stat, keys_t, vals_t, pair, own_st, sib_out, sib_in,
+    dkv_out, dkv_in, home_out, home_in, total_kv, select, piece, got, red, fin,
+    load_sem,
     low_send, low_recv, dlow_send, dlow_recv,
-    col_send, row_send, kv_recv, fwd_send, fwd_recv, sib_send, sib_recv, dkv_send, dkv_recv,
+    col_send, row_send, direct_send, kv_recv, fwd_send, fwd_recv, sib_send, sib_recv, dkv_send, dkv_recv,
     home_send, home_recv,
     a1_send, a1_recv, a2_send, a2_recv,
 ):
@@ -69,6 +69,9 @@
     x = chip % wide
     y = chip // wide
     earlier = jnp.minimum(reach, chip)
+
+    def at_chip(to_x, to_y):
+        return ((to_y * wide + to_x) * 2 + core, m)
 
     def load(src, dst, n):
         return pltpu.make_async_copy(src, dst, load_sem.at[n])
@@ -92,15 +95,27 @@
     partners += [((own + span * step) % seq, m) for step in range(1, seq // span)]
     for peer in partners:
         pl.semaphore_signal(barrier, inc=1, device_id=peer, device_id_type=MESH)
+    skips = wide - 1
+    greeted = len(partners)
+    if skips:
+        greeted += jnp.where(x == skips, jnp.minimum(2, tall - 1 - y), 0)
+        for dy in range(1, 3):
+
+            @pl.when(jnp.logical_and(x == 0, y >= dy))
+            def _():
+                pl.semaphore_signal(
+                    barrier, inc=1, device_id=at_chip(skips, y - dy), device_id_type=MESH
+                )
+
     for n in (7, 8, 2, 3, 6, 4, 5):
         loads[n].start()
     loads[0].wait()
     loads[1].wait()
-    pl.semaphore_wait(barrier, len(partners))
+    pl.semaphore_wait(barrier, greeted)
 
     def exchange(buf, send, recv):
         copies = []
-        for step in range(1, mp):
+        for step in sorted(range(1, mp), key=lambda step: abs(step - mp // 2)):
             peer = (m + step) % mp
             copies.append(
                 pltpu.make_async_remote_copy(
@@ -111,9 +126,6 @@
             )
         return copies
 
-    def at_chip(to_x, to_y):
-        return ((to_y * wide + to_x) * 2 + core, m)
-
     def column_copy(dy):
         return pltpu.make_async_remote_copy(
             src_ref=kv.at[0, :, mine], dst_ref=kv.at[dy * wide, :, mine],
@@ -121,6 +133,21 @@
             device_id=at_chip(x, y + dy), device_id_type=MESH,
         )
 
+    def direct_copy(dy):
+        e = dy * wide - skips
+        return pltpu.make_async_remote_copy(
+            src_ref=kv.at[0, :, mine], dst_ref=kv.at[e, :, mine],
+            send_sem=direct_send.at[dy], recv_sem=kv_recv.at[e],
+            device_id=at_chip(0, y + dy), device_id_type=MESH,
+        )
+
+    def direct(dy, act):
+        if skips:
+
+            @pl.when(jnp.logical_and(x == skips, y + dy < tall))
+            def _():
+                act(direct_copy(dy))
+
     def row_copy(dy, to_x):
         return pltpu.make_async_remote_copy(
             src_ref=kv.at[dy * wide, :, mine], dst_ref=kv.at[dy * wide + to_x - x, :, mine],
@@ -131,6 +158,8 @@
     def row_readers(dy, act):
         for to_x in range(wide):
             reads = (to_x > x, to_x != x, to_x < x)[dy]
+            if dy and to_x == 0:
+                reads = jnp.logical_and(reads, x != skips)
 
             @pl.when(jnp.logical_and(y >= dy, reads))
             def _():
@@ -193,6 +222,8 @@
     def _():
         column_copy(2).start()
 
+    for dy in range(1, 3):
+        direct(dy, lambda copy: copy.start())
     loads[6].wait()
     for h in range(heads):
         here = slice(h * BLK, (h + 1) * BLK)
@@ -217,7 +248,8 @@
     def _(e):
         sbuf[e] = jnp.full(sbuf.shape[1:], NEG, F32)
         dpbuf[e] = jnp.zeros(dpbuf.shape[1:], F32)
-        kv[e] = jnp.zeros(kv.shape[1:], BF16)
+        keys_t[e] = jnp.zeros(keys_t.shape[1:], BF16)
+        vals_t[e] = jnp.zeros(vals_t.shape[1:], BF16)
 
     for dy in range(1, 3):
 
@@ -257,6 +289,8 @@
         low_edge = (first - 2 * (chip - e)) * BLK
         keys = kv[e, 0]
         values = kv[e, 1]
+        keys_t[e] = keys.T
+        vals_t[e] = values.T
         for at in range(0, cols, CHUNK):
             part = slice(at, at + CHUNK)
             s = dot(keys, qt[:, part])
@@ -309,24 +343,22 @@
     stat[16:17, :] = stat[16:17, :] / total
     for e in range(units):
         here = slice(e * 2 * BLK, (e + 1) * 2 * BLK)
-        keys_t[:, here] = kv[e, 0].T
-        vals_t[:, here] = kv[e, 1].T
         for at in range(0, cols, NARROW):
             part = slice(at, at + NARROW)
             p = jnp.exp2(sbuf[e, :, part] * fold - stat[24:25, part])
             dsbuf[here, part] = (p * (dpbuf[e, :, part] - stat[16:17, part])).astype(BF16)
             pbuf[here, part] = p.astype(BF16)
-    dq_t = dot(keys_t[...], dsbuf[...]) * scale
+    def all_units(turned):
+        return jnp.concatenate([turned[e] for e in range(units)], axis=1)
+
+    dq_t = dot(all_units(keys_t), dsbuf[...]) * scale
     for h in range(heads):
         part = slice(h * HEAD, (h + 1) * HEAD)
-        gqv[:, part] = dq_t[:, part].T.astype(BF16)
-
+        gqv[:, part] = dq_t[:, h * BLK : (h + 1) * BLK].T.astype(BF16)
     dlowx[m] = dot_nt(up_rows, gqv[...])
     dlow_copies = exchange(dlowx, dlow_send, dlow_recv)
     for one in dlow_copies:
         one.start()
-    gq_copy = pltpu.make_async_copy(gqv, gq_h, out_sem.at[1])
-    gq_copy.start()
 
     own16 = pl.ds(pl.multiple_of(own * RANK, RANK), RANK)
     place16 = pl.ds(pl.multiple_of(place * RANK, RANK), RANK)
@@ -352,9 +384,9 @@
         got[kind, place16, :] = piece[kind, place]
         red[kind] = dot(select[...], got[kind]).astype(BF16)
 
-        @pl.loop(1, seq)
+        @pl.loop(0, seq - 1)
         def _(step):
-            peer = (own + step) % seq
+            peer = (own + 1 + (step + seq // 2 - 1) % (seq - 1)) % seq
             pltpu.make_async_remote_copy(
                 src_ref=red.at[kind, pl.ds(pl.multiple_of(peer * RANK, RANK), RANK)],
                 dst_ref=fin.at[kind, own16],
@@ -371,7 +403,7 @@
             for line in range(seq // span):
                 at = (line * span + t) * RANK
                 whole = whole + fin[kind, at : at + RANK, :].astype(F32)
-            gout[kind, :, t * 128 : (t + 1) * 128] = whole
+            (gb, ga)[kind][0, :, t * 128 : (t + 1) * 128] = whole
 
     def sib_copy(g):
         return pltpu.make_async_remote_copy(
@@ -455,12 +487,10 @@
     pass_on(0)
     settle(0)
 
-    out_t = dot(vals_t[...], pbuf[...])
+    out_t = dot(all_units(vals_t), pbuf[...])
     for h in range(heads):
         part = slice(h * HEAD, (h + 1) * HEAD)
         outv[:, part] = out_t[:, part].T.astype(BF16)
-    out_copy = pltpu.make_async_copy(outv, out_h, out_sem.at[0])
-    out_copy.start()
 
     def send_home(dy):
         merge_row(dy)
@@ -475,8 +505,6 @@
     send_home(1)
     merge_row(0)
     finish(0)
-    gb_copy = pltpu.make_async_copy(gout.at[0], gb_h.at[0], out_sem.at[4])
-    gb_copy.start()
     for dy in range(1, 3):
 
         @pl.when(y + dy < tall)
@@ -484,15 +512,10 @@
             home_copy(dy).wait_recv()
             total_kv[0] = total_kv[0] + home_in[dy].astype(F32)
 
-    gkv[...] = total_kv[0].astype(BF16)
-    gk_copy = pltpu.make_async_copy(gkv.at[0], gk_h, out_sem.at[2])
-    gv_copy = pltpu.make_async_copy(gkv.at[1], gv_h, out_sem.at[3])
-    gk_copy.start()
-    gv_copy.start()
+    gk[...] = total_kv[0, 0].astype(BF16)
+    gv[...] = total_kv[0, 1].astype(BF16)
 
     finish(1)
-    ga_copy = pltpu.make_async_copy(gout.at[1], ga_h.at[0], out_sem.at[5])
-    ga_copy.start()
 
     for one in low_copies + dlow_copies:
         one.wait_send()
@@ -508,6 +531,9 @@
     @pl.when(y + 2 < tall)
     def _():
         column_copy(2).wait_send()
+
+    for dy in range(1, 3):
+        direct(dy, lambda copy: copy.wait_send())
 
     @pl.loop(0, earlier + 1)
     def _(e):
@@ -528,21 +554,16 @@
         pltpu.make_async_copy(sent, sent, a1_send.at[kind]).wait()
         sent = red.at[kind, rest2]
         pltpu.make_async_copy(sent, sent, a2_send.at[kind]).wait()
-    for one in (out_copy, gq_copy, gk_copy, gv_copy, ga_copy, gb_copy):
-        one.wait()
 
 
 def place_kernel(count, *refs):
-    sources, targets, held = refs[:count], refs[count : 2 * count], refs[2 * count : 3 * count]
-    in_sem, out_sem = refs[3 * count :]
-    ins = [pltpu.make_async_copy(sources[n], held[n], in_sem.at[n]) for n in range(count)]
-    outs = [pltpu.make_async_copy(held[n], targets[n], out_sem.at[n]) for n in range(count)]
-    for one in ins:
+    sems = refs[2 * count]
+    copies = [
+        pltpu.make_async_copy(refs[n], refs[count + n], sems.at[n]) for n in range(count)
+    ]
+    for one in copies:
         one.start()
-    for came, goes in zip(ins, outs):
-        came.wait()
-        goes.start()
-    for one in outs:
+    for one in copies:
         one.wait()
 
 
@@ -572,9 +593,9 @@
     )
     made = pl.pallas_call(
         functools.partial(kernel, seq, mp, docs),
-        out_shape=shapes,
+        out_shape=[vmem(one.shape, one.dtype) for one in shapes],
         in_specs=[any_space] * 9,
-        out_specs=[any_space] * 6,
+        out_specs=[pl.BlockSpec(memory_space=pltpu.VMEM)] * 6,
         scratch_shapes=[
             pltpu.SMEM((docs,), jnp.int32),
             pltpu.SMEM((docs,), jnp.int32),
@@ -595,10 +616,8 @@
             vmem((mp, RANK, rows), F32),
             vmem((mp, RANK, rows), F32),
             vmem((32, cols), F32),
-            vmem((HEAD, units * 2 * BLK), BF16),
-            vmem((HEAD, units * 2 * BLK), BF16),
-            vmem((rows, cols), BF16),
-            vmem((rows, cols), BF16),
+            vmem((units, HEAD, 2 * BLK), BF16),
+            vmem((units, HEAD, 2 * BLK), BF16),
             vmem((2, GROUP * 2 * BLK, HEAD), F32),
             vmem((groups, GROUP, 2, BLK, HEAD), F32),
             vmem((groups, GROUP, 2, BLK, HEAD), BF16),
@@ -607,36 +626,38 @@
             vmem((3, wide, 2, BLK, HEAD), BF16),
             vmem((3, 2, BLK, HEAD), BF16),
             vmem((3, 2, BLK, HEAD), BF16),
-            vmem((2, BLK, HEAD), BF16),
             vmem((3, 2, BLK, HEAD), F32),
             vmem((adapters * RANK, span * RANK), BF16),
             vmem((2, span, RANK, 128), BF16),
             vmem((2, span * RANK, 128), BF16),
             vmem((2, seq * RANK, 128), BF16),
             vmem((2, seq * RANK, 128), BF16),
-            vmem((2, RANK, cols), F32),
-            dma((9,)), dma((6,)),
+            dma((9,)),
             dma((mp,)), dma((mp,)), dma((mp,)), dma((mp,)),
-            dma((3,)), dma((3, wide)), dma((units,)), dma((units,)), dma((units,)),
+            dma((3,)), dma((3, wide)), dma((3,)), dma((units,)), dma((units,)), dma((units,)),
             dma((groups,)), dma((groups,)), dma((units,)), dma((3, wide)),
             dma((3,)), dma((3,)),
             dma((2,)), dma((2,)), dma((2,)), dma((2,)),
         ],
         compiler_params=pltpu.CompilerParams(
-            collective_id=0, has_side_effects=True, vmem_limit_bytes=63 * 1024 * 1024
+            collective_id=0, has_side_effects=True, vmem_limit_bytes=48 * 1024 * 1024
         ),
     )(
-        document_blocks, document_adapter, hidden_rows, rotated_queries, rotated_keys,
-        value_rows, adapter_down, adapter_up, output_gradient,
+        *(
+            pltpu.with_memory_space_constraint(one, pltpu.HBM)
+            for one in (
+                document_blocks, document_adapter, hidden_rows, rotated_queries, rotated_keys,
+                value_rows, adapter_down, adapter_up, output_gradient,
+            )
+        )
     )
     return pl.pallas_call(
         functools.partial(place_kernel, len(shapes)),
         out_shape=shapes,
         in_specs=[any_space] * len(shapes),
         out_specs=[any_space] * len(shapes),
-        scratch_shapes=[vmem(one.shape, one.dtype) for one in shapes]
-        + [dma((len(shapes),)), dma((len(shapes),))],
-    )(*made)
+        scratch_shapes=[dma((len(shapes),))],
+    )(*(pltpu.with_memory_space_constraint(one, pltpu.VMEM) for one in made))
 
 
 def solution(mesh):

time: 47.6 us -> 44.3 us (0.931)
  Pallas kernels: 46.8 us -> 43.6 us
    pallas_call x1, Pallas kernels: 44.9 us -> 42.7 us  [on_device(): pl.pallas_call(functools.partial(kernel, seq, mp, docs), out_shape=[vmem(...]
    pallas_call x1, Pallas kernels: 1.9 us -> 0.9 us  [on_device(): pl.pallas_call(functools.partial(place_kernel, len(shapes)), out_shape=sh...]
where the time goes in v3:
time: 44.3 us; the launch traced here: 44.2 us
  Pallas kernels  43.6 us (98%)
  between operations  0.64 us (1%)
    pallas_call x1, Pallas kernels, on_device(): pl.pallas_call(functools.partial(kernel, seq, mp, docs), out_shape=[vmem(...  42.7 us
    pallas_call x1, Pallas kernels, on_device(): pl.pallas_call(functools.partial(place_kernel, len(shapes)), out_shape=sh...  0.9 us

profile of v3, /device:TPU:1, one launch (start us, length us, event | category | flops | bytes accessed | tf_op | source)
XLA Modules:
  0.0 44.2 jit_solution(14825014172975734604)
XLA Ops:
  0.6 42.7 %shard_map.136 = (bf16[128,1024]{1,0:T(8,128)(2,1)S(1)}, bf16[128,1024]{1,0:T(8,128)(2,1)S(1)}, bf16[128,128]{1,0:T(8,128)(2,1)S(1)}, bf16[128,128]{1,0:T(8,128)...) custom-call(s32[9]{0:T(128)} %db_h.1, s32[9]{0:T(128)} %da_h.1, bf16[128,1024]{1,0:T(8,128)(2,1)} %hid_h.1, ...), custom_call_target="tpu_custom_call" | custom-call | tf_op jit(solution)/shard_map/pallas_call | solution.py:594
  43.3 0.9 %shard_map.137 = (bf16[128,1024]{1,0:T(8,128)(2,1)}, bf16[128,1024]{1,0:T(8,128)(2,1)}, bf16[128,128]{1,0:T(8,128)(2,1)}, bf16[128,128]{1,0:T(8,128)(2,1)}, f32[...) custom-call(bf16[128,1024]{1,0:T(8,128)(2,1)S(1)} %get-tuple-element.12.refs_0_, ...), custom_call_target="tpu_custom_call" | custom-call | tf_op jit(solution)/shard_map/pallas_call | solution.py:654

commit v4 on v3

--- a/solution.py
+++ b/solution.py
@@ -11,10 +11,8 @@
 HEAD = 128
 BLK = 128
 RANK = 16
-CHUNK = 1024
 NARROW = 256
 GROUP = 3
-LAG = 3
 NEG = -1e30
 LOG2E = 1.4426950408889634
 MESH = pl.DeviceIdType.MESH
@@ -37,7 +35,7 @@
     db_h, da_h, hid_h, rq_h, k_h, v_h, down_h, up_h, do_h,
     outv, gqv, gk, gv, ga, gb,
     db, da, hid, rq, down, up, do, kv, qs, qt, dos, dot_t, sbuf, dpbuf, pbuf, dsbuf,
-    lowx, dlowx, stat, keys_t, vals_t, pair, own_st, sib_out, sib_in,
+    lowx, dlowx, stat, shifts, keys_t, vals_t, pair, own_st, sib_out, sib_in,
     dkv_out, dkv_in, home_out, home_in, total_kv, select, piece, got, red, fin,
     load_sem,
     low_send, low_recv, dlow_send, dlow_recv,
@@ -64,8 +62,8 @@
     sib = own + 1 - 2 * core
     place = own % span
     base = own - place
-    mine = pl.ds(pl.multiple_of(core * BLK, BLK), BLK)
-    other = pl.ds(pl.multiple_of((1 - core) * BLK, BLK), BLK)
+    mine = slice(0, BLK)
+    other = slice(BLK, 2 * BLK)
     x = chip % wide
     y = chip // wide
     earlier = jnp.minimum(reach, chip)
@@ -174,7 +172,7 @@
 
     def forward(e):
         return pltpu.make_async_remote_copy(
-            src_ref=kv.at[e, :, mine], dst_ref=kv.at[e, :, mine],
+            src_ref=kv.at[e, :, mine], dst_ref=kv.at[e, :, other],
             send_sem=fwd_send.at[e], recv_sem=fwd_recv.at[e],
             device_id=(sib, m), device_id_type=MESH,
         )
@@ -246,10 +244,7 @@
 
     @pl.loop(earlier + 1, units)
     def _(e):
-        sbuf[e] = jnp.full(sbuf.shape[1:], NEG, F32)
-        dpbuf[e] = jnp.zeros(dpbuf.shape[1:], F32)
-        keys_t[e] = jnp.zeros(keys_t.shape[1:], BF16)
-        vals_t[e] = jnp.zeros(vals_t.shape[1:], BF16)
+        kv[e] = jnp.zeros(kv.shape[1:], BF16)
 
     for dy in range(1, 3):
 
@@ -282,72 +277,101 @@
         qs[here, :] = q
         qt[:, here] = q.T
 
-    u_rows = lax.broadcasted_iota(jnp.int32, (2 * BLK, CHUNK), 0)
-    t_cols = lax.broadcasted_iota(jnp.int32, (2 * BLK, CHUNK), 1) % BLK
-
-    def score_unit(e, diagonal):
-        low_edge = (first - 2 * (chip - e)) * BLK
-        keys = kv[e, 0]
-        values = kv[e, 1]
-        keys_t[e] = keys.T
-        vals_t[e] = values.T
-        for at in range(0, cols, CHUNK):
-            part = slice(at, at + CHUNK)
-            s = dot(keys, qt[:, part])
-            keep = u_rows >= low_edge
-            if diagonal:
-                keep = jnp.logical_and(keep, u_rows <= core * BLK + t_cols)
-            s = jnp.where(keep, s, NEG)
-            sbuf[e, :, part] = s
-            dp = dot(values, dot_t[:, part])
-            dpbuf[e, :, part] = dp
-            top = jnp.max(s, axis=0, keepdims=True)
-            if not diagonal:
-                was = stat[0:1, part]
-                top = jnp.maximum(top, was)
-            p = jnp.exp2(s * fold - top * fold)
-            total = jnp.sum(p, axis=0, keepdims=True)
-            delta = jnp.sum(p * dp, axis=0, keepdims=True)
-            if not diagonal:
-                shrink = jnp.exp2((was - top) * fold)
-                total = total + shrink * stat[8:9, part]
-                delta = delta + shrink * stat[16:17, part]
-            stat[0:1, part] = top
-            stat[8:9, part] = total
-            stat[16:17, part] = delta
+    below = lax.broadcasted_iota(jnp.int32, (BLK, cols), 0) <= (
+        lax.broadcasted_iota(jnp.int32, (BLK, cols), 1) % BLK
+    )
+    turn_of = {}
+
+    def score(turn, halves):
+        keys = jnp.concatenate([kv[e, 0, h * BLK : (h + 1) * BLK] for e, h in halves], axis=0)
+        values = jnp.concatenate([kv[e, 1, h * BLK : (h + 1) * BLK] for e, h in halves], axis=0)
+        s_all = dot(keys, qt[...])
+        dp_all = dot(values, dot_t[...])
+        keys_all = keys.T
+        values_all = values.T
+        parts = []
+        top = None if turn == 0 else stat[0:1, :]
+        for n, (e, h) in enumerate(halves):
+            turn_of[e, h] = turn
+            here = slice(n * BLK, (n + 1) * BLK)
+            half = slice(h * BLK, (h + 1) * BLK)
+            keys_t[e, :, half] = keys_all[:, here]
+            vals_t[e, :, half] = values_all[:, here]
+            block = 2 * (chip - e) + (core if h == 0 else 1 - core)
+            seen = jnp.logical_and(block >= first, block <= own)
+            s = s_all[here]
+            if e == 0 and h == 0:
+                s = jnp.where(below, s, NEG)
+            off = jnp.where(seen, 0.0, -NEG)
+            high = jnp.max(s, axis=0, keepdims=True) - off
+            top = high if top is None else jnp.maximum(top, high)
+            parts.append((e, half, s, dp_all[here], off))
+        shift = top * fold
+        total = delta = None
+        if turn:
+            shrink = jnp.exp2(stat[0:1, :] * fold - shift)
+            total = shrink * stat[8:9, :]
+            delta = shrink * stat[16:17, :]
+        for e, half, s, dp, off in parts:
+            p = jnp.exp2(s * fold - (shift + off))
+            sbuf[e, half, :] = p
+            dpbuf[e, half, :] = dp
+            row_sum = jnp.sum(p, axis=0, keepdims=True)
+            row_delta = jnp.sum(p * dp, axis=0, keepdims=True)
+            total = row_sum if total is None else total + row_sum
+            delta = row_delta if delta is None else delta + row_delta
+        stat[0:1, :] = top
+        stat[8:9, :] = total
+        stat[16:17, :] = delta
+        shifts[turn : turn + 1, :] = shift
 
     forward_land(0).wait_recv()
-    score_unit(0, True)
-
     for dy in range(1, 3):
 
         @pl.when(y >= dy)
         def _():
             forward_land(dy * wide).wait_recv()
-            score_unit(dy * wide, False)
-
-    @pl.loop(1, earlier + 1 + LAG)
-    def _(e):
-        @pl.when(jnp.logical_and(jnp.logical_and(e > x, e <= earlier), e % wide != 0))
-        def _():
-            kv_land(e).wait_recv()
-            forward(e).start()
-
-        @pl.when(jnp.logical_and(e > LAG, (e - LAG) % wide != 0))
-        def _():
-            forward_land(e - LAG).wait_recv()
-            score_unit(e - LAG, False)
+
+    score(0, [(dy * wide, h) for dy in range(3) for h in range(2)])
+    turns = 1
+    for dy in range(2):
+        near = [dy * wide + step for step in range(1, wide)]
+        for e in near:
+
+            @pl.when(jnp.logical_and(e > x, e <= earlier))
+            def _():
+                kv_land(e).wait_recv()
+                forward(e).start()
+
+        if near:
+            score(turns, [(e, 0) for e in near])
+        for e in near:
+
+            @pl.when(e <= earlier)
+            def _():
+                forward_land(e).wait_recv()
+
+        if near:
+            score(turns + 1, [(e, 1) for e in near])
+        turns += 2
 
     total = stat[8:9, :]
-    stat[24:25, :] = stat[0:1, :] * fold + jnp.log(total) * LOG2E
+    shifts[8:16, :] = jnp.exp2(
+        shifts[0:8, :] - (stat[0:1, :] * fold + jnp.log(total) * LOG2E)
+    )
     stat[16:17, :] = stat[16:17, :] / total
     for e in range(units):
-        here = slice(e * 2 * BLK, (e + 1) * 2 * BLK)
-        for at in range(0, cols, NARROW):
-            part = slice(at, at + NARROW)
-            p = jnp.exp2(sbuf[e, :, part] * fold - stat[24:25, part])
-            dsbuf[here, part] = (p * (dpbuf[e, :, part] - stat[16:17, part])).astype(BF16)
-            pbuf[here, part] = p.astype(BF16)
+        for h in range(2):
+            half = slice(h * BLK, (h + 1) * BLK)
+            here = slice((2 * e + h) * BLK, (2 * e + h + 1) * BLK)
+            factor = 8 + turn_of[e, h]
+            for at in range(0, cols, NARROW):
+                part = slice(at, at + NARROW)
+                p = sbuf[e, half, part] * shifts[factor : factor + 1, part]
+                ds = p * (dpbuf[e, half, part] - stat[16:17, part])
+                dsbuf[here, part] = ds.astype(BF16)
+                pbuf[here, part] = p.astype(BF16)
+
     def all_units(turned):
         return jnp.concatenate([turned[e] for e in range(units)], axis=1)
 
@@ -451,10 +475,9 @@
         pair[1] = dot(pbuf[here, :], dos[...])
         for k in range(GROUP):
             for kind in range(2):
-                lower = pl.ds(pl.multiple_of((2 * k + core) * BLK, BLK), BLK)
-                upper = pl.ds(pl.multiple_of((2 * k + 1 - core) * BLK, BLK), BLK)
-                own_st[g, k, kind] = pair[kind, lower, :]
-                sib_out[g, k, kind] = pair[kind, upper, :].astype(BF16)
+                at = 2 * k * BLK
+                own_st[g, k, kind] = pair[kind, at : at + BLK, :]
+                sib_out[g, k, kind] = pair[kind, at + BLK : at + 2 * BLK, :].astype(BF16)
         sib_copy(g).start()
 
     def pass_on(g):
@@ -615,7 +638,8 @@
             vmem((units * 2 * BLK, cols), BF16),
             vmem((mp, RANK, rows), F32),
             vmem((mp, RANK, rows), F32),
-            vmem((32, cols), F32),
+            vmem((24, cols), F32),
+            vmem((16, cols), F32),
             vmem((units, HEAD, 2 * BLK), BF16),
             vmem((units, HEAD, 2 * BLK), BF16),
             vmem((2, GROUP * 2 * BLK, HEAD), F32),

time: 44.3 us -> 43.8 us (0.989)
  Pallas kernels: 43.6 us -> 43 us
    pallas_call x1, Pallas kernels: 42.7 us -> 42.1 us  [on_device(): pl.pallas_call(functools.partial(kernel, seq, mp, docs), out_shape=[vmem(...]
where the time goes in v4:
time: 43.8 us; the launch traced here: 43.7 us
  Pallas kernels  43 us (98%)
  between operations  0.64 us (1%)
    pallas_call x1, Pallas kernels, on_device(): pl.pallas_call(functools.partial(kernel, seq, mp, docs), out_shape=[vmem(...  42.1 us
    pallas_call x1, Pallas kernels, on_device(): pl.pallas_call(functools.partial(place_kernel, len(shapes)), out_shape=sh...  0.9 us

profile of v4, /device:TPU:1, one launch (start us, length us, event | category | flops | bytes accessed | tf_op | source)
XLA Modules:
  0.0 43.7 jit_solution(13197908712643088064)
XLA Ops:
  0.6 42.1 %shard_map.136 = (bf16[128,1024]{1,0:T(8,128)(2,1)S(1)}, bf16[128,1024]{1,0:T(8,128)(2,1)S(1)}, bf16[128,128]{1,0:T(8,128)(2,1)S(1)}, bf16[128,128]{1,0:T(8,128)...) custom-call(s32[9]{0:T(128)} %db_h.1, s32[9]{0:T(128)} %da_h.1, bf16[128,1024]{1,0:T(8,128)(2,1)} %hid_h.1, ...), custom_call_target="tpu_custom_call" | custom-call | tf_op jit(solution)/shard_map/pallas_call | solution.py:617
  42.8 0.9 %shard_map.137 = (bf16[128,1024]{1,0:T(8,128)(2,1)}, bf16[128,1024]{1,0:T(8,128)(2,1)}, bf16[128,128]{1,0:T(8,128)(2,1)}, bf16[128,128]{1,0:T(8,128)(2,1)}, f32[...) custom-call(bf16[128,1024]{1,0:T(8,128)(2,1)S(1)} %get-tuple-element.12.refs_0_, ...), custom_call_target="tpu_custom_call" | custom-call | tf_op jit(solution)/shard_map/pallas_call | solution.py:678

commit v5 on v4

--- a/solution.py
+++ b/solution.py
@@ -60,12 +60,16 @@
     chip = own // 2
     core = own % 2
     sib = own + 1 - 2 * core
-    place = own % span
-    base = own - place
     mine = slice(0, BLK)
     other = slice(BLK, 2 * BLK)
     x = chip % wide
     y = chip // wide
+    tier = span // 2
+    place = (y % tier) * 2 + core
+    level = y - y % tier
+
+    def member(p):
+        return ((level + p // 2) * wide + x) * 2 + p % 2
     earlier = jnp.minimum(reach, chip)
 
     def at_chip(to_x, to_y):
@@ -89,8 +93,10 @@
     loads[1].start()
     barrier = pltpu.get_barrier_semaphore()
     partners = [(own, (m + step) % mp) for step in range(1, mp)]
-    partners += [(base + (place + step) % span, m) for step in range(1, span)]
-    partners += [((own + span * step) % seq, m) for step in range(1, seq // span)]
+    partners += [(sib, m)]
+    partners += [at_chip(x, (y + step) % tall) for step in range(1, tall)]
+    partners += [(member((place + 2 * step + 1 - 2 * core) % span), m) for step in range(1, tier)]
+    partners += [at_chip((x + step) % wide, y) for step in range(1, wide)]
     for peer in partners:
         pl.semaphore_signal(barrier, inc=1, device_id=peer, device_id_type=MESH)
     skips = wide - 1
@@ -234,7 +240,7 @@
     col = lax.broadcasted_iota(jnp.int32, size, 1)
     same = (row % RANK) == (col % RANK)
     row_a = row // RANK
-    col_s = base + col // RANK
+    col_s = member(col // RANK)
     hit = jnp.zeros(size, F32)
     for begin, end, name in bounds:
         inside = jnp.logical_and(col_s >= begin, col_s < end)
@@ -370,7 +376,6 @@
                 p = sbuf[e, half, part] * shifts[factor : factor + 1, part]
                 ds = p * (dpbuf[e, half, part] - stat[16:17, part])
                 dsbuf[here, part] = ds.astype(BF16)
-                pbuf[here, part] = p.astype(BF16)
 
     def all_units(turned):
         return jnp.concatenate([turned[e] for e in range(units)], axis=1)
@@ -399,7 +404,7 @@
             pltpu.make_async_remote_copy(
                 src_ref=piece.at[kind, peer], dst_ref=got.at[kind, place16],
                 send_sem=a1_send.at[kind], recv_sem=a1_recv.at[kind],
-                device_id=(base + peer, m), device_id_type=MESH,
+                device_id=(member(peer), m), device_id_type=MESH,
             ).start()
 
     def settle(kind):
@@ -408,9 +413,9 @@
         got[kind, place16, :] = piece[kind, place]
         red[kind] = dot(select[...], got[kind]).astype(BF16)
 
-        @pl.loop(0, seq - 1)
-        def _(step):
-            peer = (own + 1 + (step + seq // 2 - 1) % (seq - 1)) % seq
+        for step in sorted(range(1, seq), key=lambda step: abs(step - seq // 2 - wide // 2)):
+            peer = own + step
+            peer = jnp.where(peer >= seq, peer - seq, peer)
             pltpu.make_async_remote_copy(
                 src_ref=red.at[kind, pl.ds(pl.multiple_of(peer * RANK, RANK), RANK)],
                 dst_ref=fin.at[kind, own16],
@@ -425,7 +430,8 @@
         for t in range(span):
             whole = jnp.zeros((RANK, 128), F32)
             for line in range(seq // span):
-                at = (line * span + t) * RANK
+                line_y = line // wide * tier + t // 2
+                at = ((line_y * wide + line % wide) * 2 + t % 2) * RANK
                 whole = whole + fin[kind, at : at + RANK, :].astype(F32)
             (gb, ga)[kind][0, :, t * 128 : (t + 1) * 128] = whole
 
@@ -469,7 +475,19 @@
                 merge_land(dy, from_x).wait_recv()
                 total_kv[dy] = total_kv[dy] + dkv_in[dy, from_x].astype(F32)
 
+    def fix(g):
+        for e in range(g * GROUP, (g + 1) * GROUP):
+            for h in range(2):
+                half = slice(h * BLK, (h + 1) * BLK)
+                here = slice((2 * e + h) * BLK, (2 * e + h + 1) * BLK)
+                factor = 8 + turn_of[e, h]
+                for at in range(0, cols, NARROW):
+                    part = slice(at, at + NARROW)
+                    p = sbuf[e, half, part] * shifts[factor : factor + 1, part]
+                    pbuf[here, part] = p.astype(BF16)
+
     def weigh(g):
+        fix(g)
         here = slice(g * GROUP * 2 * BLK, (g + 1) * GROUP * 2 * BLK)
         pair[0] = dot(dsbuf[here, :], qs[...]) * scale
         pair[1] = dot(pbuf[here, :], dos[...])
@@ -495,11 +513,13 @@
                 def _():
                     copy.start()
 
-    spread(0, dot(low_t, gqv[...]))
     for g in range(groups - 1, -1, -1):
         weigh(g)
+        if g == groups - 2 or groups == 1:
+            spread(0, dot(low_t, gqv[...]))
         if g < groups - 1:
             pass_on(g + 1)
+    pass_on(0)
 
     for one in dlow_copies:
         one.wait_recv()
@@ -507,7 +527,6 @@
     for step in range(1, mp):
         dlow_sum = dlow_sum + dlowx[step]
     spread(1, dot(dlow_sum.astype(BF16), hid[...]))
-    pass_on(0)
     settle(0)
 
     out_t = dot(all_units(vals_t), pbuf[...])

time: 43.8 us -> 42.5 us (0.970)
  Pallas kernels: 43 us -> 41.7 us
    pallas_call x1, Pallas kernels: 42.1 us -> 40.8 us  [on_device(): pl.pallas_call(functools.partial(kernel, seq, mp, docs), out_shape=[vmem(...]
where the time goes in v5:
time: 42.5 us; the launch traced here: 42.4 us
  Pallas kernels  41.7 us (98%)
  between operations  0.64 us (2%)
    pallas_call x1, Pallas kernels, on_device(): pl.pallas_call(functools.partial(kernel, seq, mp, docs), out_shape=[vmem(...  40.8 us
    pallas_call x1, Pallas kernels, on_device(): pl.pallas_call(functools.partial(place_kernel, len(shapes)), out_shape=sh...  0.9 us

profile of v5, /device:TPU:1, one launch (start us, length us, event | category | flops | bytes accessed | tf_op | source)
XLA Modules:
  0.0 42.4 jit_solution(8958121232990739416)
XLA Ops:
  0.6 40.8 %shard_map.136 = (bf16[128,1024]{1,0:T(8,128)(2,1)S(1)}, bf16[128,1024]{1,0:T(8,128)(2,1)S(1)}, bf16[128,128]{1,0:T(8,128)(2,1)S(1)}, bf16[128,128]{1,0:T(8,128)...) custom-call(s32[9]{0:T(128)} %db_h.1, s32[9]{0:T(128)} %da_h.1, bf16[128,1024]{1,0:T(8,128)(2,1)} %hid_h.1, ...), custom_call_target="tpu_custom_call" | custom-call | tf_op jit(solution)/shard_map/pallas_call | solution.py:636
  41.5 0.9 %shard_map.137 = (bf16[128,1024]{1,0:T(8,128)(2,1)}, bf16[128,1024]{1,0:T(8,128)(2,1)}, bf16[128,128]{1,0:T(8,128)(2,1)}, bf16[128,128]{1,0:T(8,128)(2,1)}, f32[...) custom-call(bf16[128,1024]{1,0:T(8,128)(2,1)S(1)} %get-tuple-element.12.refs_0_, ...), custom_call_target="tpu_custom_call" | custom-call | tf_op jit(solution)/shard_map/pallas_call | solution.py:697

commit v6 on v5

--- a/solution.py
+++ b/solution.py
@@ -24,6 +24,10 @@
 
 def dot(a, b):
     return jnp.dot(a, b, preferred_element_type=F32)
+
+
+def wrap(value, size):
+    return jnp.where(value >= size, value - size, value)
 
 
 def dot_nt(a, b):
@@ -92,11 +96,11 @@
     loads[0].start()
     loads[1].start()
     barrier = pltpu.get_barrier_semaphore()
-    partners = [(own, (m + step) % mp) for step in range(1, mp)]
+    partners = [(own, wrap(m + step, mp)) for step in range(1, mp)]
     partners += [(sib, m)]
-    partners += [at_chip(x, (y + step) % tall) for step in range(1, tall)]
-    partners += [(member((place + 2 * step + 1 - 2 * core) % span), m) for step in range(1, tier)]
-    partners += [at_chip((x + step) % wide, y) for step in range(1, wide)]
+    partners += [at_chip(x, wrap(y + step, tall)) for step in range(1, tall)]
+    partners += [(member(wrap(place + 2 * step + 1 - 2 * core, span)), m) for step in range(1, tier)]
+    partners += [at_chip(wrap(x + step, wide), y) for step in range(1, wide)]
     for peer in partners:
         pl.semaphore_signal(barrier, inc=1, device_id=peer, device_id_type=MESH)
     skips = wide - 1
@@ -120,7 +124,7 @@
     def exchange(buf, send, recv):
         copies = []
         for step in sorted(range(1, mp), key=lambda step: abs(step - mp // 2)):
-            peer = (m + step) % mp
+            peer = wrap(m + step, mp)
             copies.append(
                 pltpu.make_async_remote_copy(
                     src_ref=buf.at[m], dst_ref=buf.at[m],
@@ -398,9 +402,8 @@
         for t in range(span):
             piece[kind, t] = product[:, t * 128 : (t + 1) * 128].astype(BF16)
 
-        @pl.loop(1, span)
-        def _(step):
-            peer = (place + step) % span
+        for step in sorted(range(1, span), key=lambda step: abs(step - span // 2)):
+            peer = wrap(place + step, span)
             pltpu.make_async_remote_copy(
                 src_ref=piece.at[kind, peer], dst_ref=got.at[kind, place16],
                 send_sem=a1_send.at[kind], recv_sem=a1_recv.at[kind],

time: 42.5 us -> 42.5 us (level)
  no operation moved by 1% of the time
where the time goes in v6:
time: 42.5 us; the launch traced here: 42.4 us
  Pallas kernels  41.7 us (98%)
  between operations  0.64 us (2%)
    pallas_call x1, Pallas kernels, on_device(): pl.pallas_call(functools.partial(kernel, seq, mp, docs), out_shape=[vmem(...  40.8 us
    pallas_call x1, Pallas kernels, on_device(): pl.pallas_call(functools.partial(place_kernel, len(shapes)), out_shape=sh...  0.9 us

profile of v6, /device:TPU:1, one launch (start us, length us, event | category | flops | bytes accessed | tf_op | source)
XLA Modules:
  0.0 42.4 jit_solution(13036859841291136258)
XLA Ops:
  0.6 40.8 %shard_map.136 = (bf16[128,1024]{1,0:T(8,128)(2,1)S(1)}, bf16[128,1024]{1,0:T(8,128)(2,1)S(1)}, bf16[128,128]{1,0:T(8,128)(2,1)S(1)}, bf16[128,128]{1,0:T(8,128)...) custom-call(s32[9]{0:T(128)} %db_h.1, s32[9]{0:T(128)} %da_h.1, bf16[128,1024]{1,0:T(8,128)(2,1)} %hid_h.1, ...), custom_call_target="tpu_custom_call" | custom-call | tf_op jit(solution)/shard_map/pallas_call | solution.py:639
  41.4 0.9 %shard_map.137 = (bf16[128,1024]{1,0:T(8,128)(2,1)}, bf16[128,1024]{1,0:T(8,128)(2,1)}, bf16[128,128]{1,0:T(8,128)(2,1)}, bf16[128,128]{1,0:T(8,128)(2,1)}, f32[...) custom-call(bf16[128,1024]{1,0:T(8,128)(2,1)S(1)} %get-tuple-element.12.refs_0_, ...), custom_call_target="tpu_custom_call" | custom-call | tf_op jit(solution)/shard_map/pallas_call | solution.py:700
